TPU v7x, 256 devices: a whole 4x4x8 slice. The times are simulated.
256 devices in a mesh: dp: 2 (over core), fsdp: 32 (over z, x), col: 4 (over y).
Axes of the slice: x: 4, y: 4, z: 8, core: 2. Of those that a mesh axis runs over, the one named last changes fastest.
Arguments:
- acts: bfloat16 [12288, 12288], P(('dp', 'fsdp'), 'col'), may hold values from -6 to 6, as said below
- cotangent: bfloat16 [2, 12288, 1024], P(None, ('dp', 'fsdp'), 'col'), may hold values from -36 to 36, as said below
- base: bfloat16 [2, 12288, 1024], P(None, 'fsdp', 'col'), may hold values from -4 to 4, as said below
- adapter_a: bfloat16 [2, 12288, 32], replicated, may hold values from -0.5 to 0.5, as said below
- adapter_b: bfloat16 [2, 32, 1024], P(None, None, 'col'), may hold values from -6 to 6
- magnitude: float32 [2, 1024], P(None, 'col'), may hold values from 0.5 to 2
Outputs:
- grad_acts: bfloat16 [12288, 12288], P(('dp', 'fsdp'), 'col')
- grad_a: float32 [2, 12288, 32], replicated
- grad_b: float32 [2, 32, 1024], P(None, None, 'col')
- grad_mag: float32 [2, 1024], P(None, 'col')
Inputs may be any that keep to these rules, and one draw needn't show every extreme that they name: `acts`: real-valued. `base`: real-valued. `cotangent`: real-valued. `adapter_a`: real-valued.
All inputs are finite; a program needn't handle non-finite values.
Results may differ from a plain program's by a relative error of at most 0.0075.
Values may be sent and summed in bfloat16 or wider, within the bound.
A program may use at most 128 MiB of HBM per device.

v0:
```python
import jax
import jax.numpy as jnp
from jax import lax
from jax.sharding import PartitionSpec as P


def on_device(acts, cotangent, base, adapter_a, adapter_b, magnitude):
    highest = lax.Precision.HIGHEST
    tok_rows = acts.shape[0]
    col_span = acts.shape[1]
    model_width = adapter_a.shape[1]
    rank_width = adapter_a.shape[2]
    shard_rows = base.shape[1]
    row_start = lax.axis_index("fsdp") * shard_rows
    col_start = lax.axis_index("col") * col_span
    lead_core = (lax.axis_index("dp") == 0).astype(jnp.float32)

    def column_stats(which):
        down_rows = lax.dynamic_slice_in_dim(adapter_a[which], row_start, shard_rows, 0)
        composed = base[which].astype(jnp.float32) + jnp.dot(
            down_rows, adapter_b[which], preferred_element_type=jnp.float32
        )
        squares = jnp.sum(composed * composed, axis=0)
        products = jnp.dot(down_rows.astype(jnp.float32).T, composed, precision=highest)
        return (composed, squares, products)

    stats_list = [column_stats(which) for which in range(2)]
    summed = [lax.psum((stats[1], stats[2]), "fsdp") for stats in stats_list]
    features = lax.all_gather(acts, "col", axis=1, tiled=True)
    input_grad = jnp.zeros((tok_rows, model_width), jnp.float32)
    low_total = jnp.zeros((tok_rows, col_span), jnp.float32)
    list_a = []
    list_b = []
    list_m = []
    for which in range(2):
        composed = stats_list[which][0]
        squares, across = summed[which]
        norms = jnp.sqrt(squares)
        scaling = magnitude[which] / norms
        cot_wide = cotangent[which].astype(jnp.float32)
        scaled = (cot_wide * scaling).astype(jnp.bfloat16)
        upper = adapter_b[which]
        upper_wide = upper.astype(jnp.float32)
        down_cols = lax.dynamic_slice_in_dim(adapter_a[which], col_start, col_span, 0)
        low_in, low_sum = lax.psum(
            (
                jnp.dot(acts, down_cols, preferred_element_type=jnp.float32),
                jnp.einsum("tj,rj->tr", scaled, upper, preferred_element_type=jnp.float32),
            ),
            "col",
        )
        low_out = low_sum.astype(jnp.bfloat16)
        piece = lax.all_gather(base[which], "fsdp", axis=0, tiled=True)
        backward = input_grad
        partial_out = jnp.dot(features, piece, preferred_element_type=jnp.float32)
        row_block = backward + jnp.einsum(
            "tj,ij->ti", scaled, piece, preferred_element_type=jnp.float32
        )
        input_grad = row_block
        full_out = partial_out + jnp.dot(low_in, upper_wide, precision=highest)
        moment, token_b = lax.psum(
            (jnp.sum(cot_wide * full_out, axis=0), jnp.dot(low_in.T, cot_wide, precision=highest)),
            ("dp", "fsdp"),
        )
        grad_mag = moment / norms
        grad_b = scaling * (token_b - across * (grad_mag / norms))
        factor = scaling * grad_mag / norms
        correction = jnp.dot(composed * factor, upper_wide.T, precision=highest)
        token_rows = jnp.einsum("td,tr->dr", acts, low_out, preferred_element_type=jnp.float32)
        adapter_term = jnp.zeros((model_width, rank_width), jnp.float32)
        adapter_term = lax.dynamic_update_slice_in_dim(adapter_term, token_rows, col_start, 0)
        rows_now = (
            lax.dynamic_slice_in_dim(adapter_term, row_start, shard_rows, 0)
            - lead_core * correction
        )
        adapter_term = lax.dynamic_update_slice_in_dim(adapter_term, rows_now, row_start, 0)
        list_a.append(lax.psum(adapter_term, ("dp", "fsdp", "col")))
        low_total = low_total + jnp.einsum(
            "tr,dr->td", low_out, down_cols, preferred_element_type=jnp.float32
        )
        list_b.append(grad_b)
        list_m.append(grad_mag)
    grad_a_all = jnp.stack(list_a)
    input_grad = lax.psum_scatter(input_grad, "col", scatter_dimension=1, tiled=True)
    grad_acts = (input_grad + low_total).astype(jnp.bfloat16)
    return (grad_acts, grad_a_all, jnp.stack(list_b), jnp.stack(list_m))


def solution(mesh):
    in_specs = (
        P(("dp", "fsdp"), "col"),
        P(None, ("dp", "fsdp"), "col"),
        P(None, "fsdp", "col"),
        P(),
        P(None, None, "col"),
        P(None, "col"),
    )
    out_specs = (P(("dp", "fsdp"), "col"), P(), P(None, None, "col"), P(None, "col"))
    return jax.shard_map(
        on_device, mesh=mesh, in_specs=in_specs, out_specs=out_specs, check_vma=False
    )
```

profile of v0, /device:TPU:1, one launch (start us, length us, event | category | flops | bytes accessed | tf_op | source)
XLA Modules:
  0.0 741.2 jit_solution(8877221594646610058)
XLA Ops:
  8.1 2.4 fusion.98
  10.5 1.8 multiply_reduce_fusion.1
  13.9 1.6 fusion.63
  18.2 1.4 convolution_bitcast_fusion.3
  19.5 150.0 %all-reduce.13.cloned.1.call-done = (f32[256]{0:T(256)}, f32[256]{0:T(256)}, f32[32,256]{1,0:T(8,128)}, f32[32,256]{1,0:T(8,128)}) async-done(((f32[256]{0:T(256)}, f32[256]{0:T(256)}, f32[32,256]{1,0:T(8,128)}, f32[32,256]{1,0:T(8,128)}), (f32[256]{0:T(256)}, f32[256]{0:T(256)}, f32[32,256]{1,0:T(8,128)}, f32[32,256]{1,0:T(8,128)})) %all-reduce.13.cloned.1.call-update) | async-done | bytes 67600 | tf_op jit(solution)/shard_map/psum | solution.py:28
  171.8 15.1 %all-reduce.14 = (bf16[192,32]{0,1:T(8,128)(2,1)}, bf16[192,32]{0,1:T(8,128)(2,1)S(1)}, f32[192,32]{0,1:T(8,128)S(1)}, f32[192,32]{0,1:T(8,128)S(1)}) all-reduce(f32[192,32]{0,1:T(8,128)S(1)} %fusion.37, f32[192,32]{0,1:T(8,128)S(1)} %fusion.40, ...), channel_id=1, replica_groups=mesh['dp'=2,'fsdp'=32,'col'=4] {'col'}, use_global_device_ids=true, to_apply=%region_5.0 | all-reduce | flops 24576 | bytes 172032 | tf_op jit(solution)/shard_map/psum | solution.py:45
  188.4 1.2 broadcast.19.clone
  189.7 1.1 fusion.9
  190.8 5.7 fusion
  197.3 58.9 %all-gather.8.cloned.1.call-done = bf16[1,12288,256]{2,1,0:T(8,128)(2,1)} async-done(((bf16[1,384,256]{2,1,0:T(8,128)(2,1)}), bf16[1,12288,256]{2,1,0:T(8,128)(2,1)}) %all-gather.8.cloned.1.call-update) | async-done | bytes 6291472 | tf_op jit(solution)/shard_map/all_gather | solution.py:53
  256.2 5.6 fusion.3
  262.9 1.0 fusion.10
  263.9 2.7 copy.23
  266.7 1.2 copy.25
  267.8 161.4 %all-reduce.11.cloned.1.call-done = (f32[256]{0:T(256)}, f32[256]{0:T(256)}, f32[32,256]{1,0:T(8,128)}, f32[32,256]{1,0:T(8,128)}) async-done(((f32[256]{0:T(256)}, f32[256]{0:T(256)}, f32[32,256]{1,0:T(8,128)}, f32[32,256]{1,0:T(8,128)}), (f32[256]{0:T(256)}, f32[256]{0:T(256)}, f32[32,256]{1,0:T(8,128)}, f32[32,256]{1,0:T(8,128)})) %all-reduce.11.cloned.1.call-update) | async-done | bytes 67600 | tf_op jit(solution)/shard_map/psum | solution.py:61
  429.2 1.2 multiply_divide_fusion.2
  430.4 1.2 multiply_divide_fusion.3
  431.7 1.8 fusion.17
  434.5 5.0 fusion.5
  439.5 8.8 %convolution_add_fusion = f32[192,12288]{1,0:T(8,128)} fusion(f32[192,12288]{1,0:T(8,128)S(1)} %fusion.5, bf16[1,12288,256]{2,1,0:T(8,128)(2,1)} %all-gather.10.cloned.1.call-done, f32[256]{0:T(256)S(1)} %copy-done.16, bf16[2,192,256]{2,1,0:T(8,128)(2,1)S(1)} %copy-done.2), kind=kOutput, calls=%fused_computation | convolution fusion | flops 1210466304 | bytes 25265152 | tf_op jit(solution)/shard_map/tj,ij->ti/dot_general | solution.py:56
  449.1 1.4 fusion.28
  451.9 274.9 %all-reduce.9.cloned.1.call-done = (f32[1,12288,32]{1,2,0:T(8,128)}, f32[1,12288,32]{1,2,0:T(8,128)}) async-done(((f32[1,12288,32]{1,2,0:T(8,128)}, f32[1,12288,32]{1,2,0:T(8,128)}), (f32[1,12288,32]{1,2,0:T(8,128)}, f32[1,12288,32]{1,2,0:T(8,128)})) %all-reduce.9.cloned.1.call-update) | async-done | bytes 3145744 | tf_op jit(solution)/shard_map/psum | solution.py:77
  726.8 3.8 pad_maximum_fusion
  730.6 3.3 fusion.8
  (85 shorter events, 13.0 us)
Async XLA Ops:
  8.0 2.5 copy-start.4
  8.0 2.5 copy-start.5
  8.0 161.6 %all-reduce.13.cloned.1.call-start = ((), (), s32[]{:S(2)}) async-start(), calls=%async_computation.7 | async-start | bytes 135168 | tf_op jit(solution)/shard_map/psum | solution.py:28
  10.5 7.7 %copy-start.3 = (bf16[1,12288,32]{1,2,0:T(8,128)(2,1)}, bf16[1,12288,32]{1,2,0:T(8,128)(2,1)S(1)}, u32[]{:S(2)}) copy-start(bf16[1,12288,32]{1,2,0:T(8,128)(2,1)S(1)} %get-tuple-element.22) | copy-start | bytes 2359300
  10.5 7.2 copy-start.24
  10.5 7.2 copy-start
  15.6 154.6 %copy-start.1 = (bf16[2,192,256]{2,1,0:T(8,128)(2,1)S(1)}, bf16[2,192,256]{2,1,0:T(8,128)(2,1)}, u32[]{:S(2)}) copy-start(bf16[2,192,256]{2,1,0:T(8,128)(2,1)} %param.7) | copy-start | bytes 589828
  15.6 175.2 %all-gather.6.cloned.1.call-start = ((), (), s32[]{:S(2)}) async-start(), calls=%async_computation.2 | async-start | bytes 5898240 | tf_op jit(solution)/shard_map/all_gather | solution.py:29
  16.2 174.6 %all-gather.10.cloned.1.call-start = ((), (), s32[]{:S(2)}) async-start(), calls=%async_computation.4 | async-start | bytes 6488064 | tf_op jit(solution)/shard_map/all_gather | solution.py:53
  17.0 239.2 %all-gather.8.cloned.1.call-start = ((), (), s32[]{:S(2)}) async-start(), calls=%async_computation.3 | async-start | bytes 6488064 | tf_op jit(solution)/shard_map/all_gather | solution.py:53
  17.6 411.6 %all-reduce.11.cloned.1.call-start = ((), (), s32[]{:S(2)}) async-start(), calls=%async_computation.6 | async-start | bytes 135168 | tf_op jit(solution)/shard_map/psum | solution.py:61
  262.7 464.1 %all-reduce.9.cloned.1.call-start = ((), (), s32[]{:S(2)}) async-start(), calls=%async_computation.5 | async-start | bytes 6291456 | tf_op jit(solution)/shard_map/psum | solution.py:77
  266.6 162.6 %copy-start.16 = (f32[256]{0:T(256)S(1)}, f32[256]{0:T(256)}, u32[]{:S(2)}) copy-start(f32[256]{0:T(256)} %copy-done.15) | copy-start | bytes 3076
  266.7 162.6 %copy-start.21 = (f32[256]{0:T(256)S(1)}, f32[256]{0:T(256)}, u32[]{:S(2)}) copy-start(f32[256]{0:T(256)} %get-tuple-element.11) | copy-start | bytes 3076
  266.7 163.8 %copy-start.13 = (f32[256]{0:T(256)S(1)}, f32[256]{0:T(256)}, u32[]{:S(2)}) copy-start(f32[256]{0:T(256)} %copy-done.12) | copy-start | bytes 3076
  266.7 163.8 %copy-start.20 = (f32[256]{0:T(256)S(1)}, f32[256]{0:T(256)}, u32[]{:S(2)}) copy-start(f32[256]{0:T(256)} %get-tuple-element.10) | copy-start | bytes 3076
  266.7 165.0 %copy-start.6 = (bf16[2,32,256]{2,1,0:T(8,128)(2,1)S(1)}, bf16[2,32,256]{2,1,0:T(8,128)(2,1)}, u32[]{:S(2)}) copy-start(bf16[2,32,256]{2,1,0:T(8,128)(2,1)} %param.10) | copy-start | bytes 98308
  267.8 166.7 %copy-start.2 = (bf16[2,192,256]{2,1,0:T(8,128)(2,1)S(1)}, bf16[2,192,256]{2,1,0:T(8,128)(2,1)}, u32[]{:S(2)}) copy-start(bf16[2,192,256]{2,1,0:T(8,128)(2,1)} %param.7) | copy-start | bytes 589828
  434.4 296.1 %reduce-scatter.2.cloned.1.call-start = ((), (), s32[]{:S(2)}) async-start(), calls=%async_computation.1 | async-start | bytes 11796480 | tf_op jit(solution)/shard_map/reduce_scatter | solution.py:84
  449.0 2.1 copy-start.8
  449.0 2.1 copy-start.9
  449.0 2.1 copy-start.10
  449.0 2.1 copy-start.11
  449.1 2.1 copy-start.14
  (8 other events, 11.5 us)
Sparse Core Ops, SparseCore 0:
  15.7 153.8 all-reduce.12
  262.8 166.3 all-reduce.10
  434.8 291.9 all-reduce.8
Sparse Core Ops, SparseCore 1:
  17.9 58.7 all-gather.5
  79.1 89.3 all-gather.9
  170.8 85.3 all-gather.7
  448.4 90.7 reduce-scatter.1
where the time goes:
time: 743 us; the launch traced here: 741 us
  waiting for transfers between devices  646 us (87%)
  matrix products  45.2 us (6%)
  between operations  15.7 us (2%)
  blocking collectives  15.1 us (2%)
  local copies, waits for them, and re-layouts  9.77 us (1%)
  other arithmetic  8.76 us (1%)
    psum x1, waiting for transfers between devices, on_device(): list_a.append(lax.psum(adapter_term, ('dp', 'fsdp', 'col')))  275 us
    psum x1, waiting for transfers between devices, on_device(): lax.psum((jnp.sum(cot_wide * full_out, axis=0), jnp.dot(low_in.T, cot_wid...  161 us
    psum x1, waiting for transfers between devices, on_device(): summed = [lax.psum((stats[1], stats[2]), 'fsdp') for stats in stats_list]  150 us
    all_gather x2, waiting for transfers between devices, on_device(): piece = lax.all_gather(base[which], 'fsdp', axis=0, tiled=True)  58.9 us
    psum x1, blocking collectives, on_device(): lax.psum((jnp.dot(acts, down_cols, preferred_element_type=jnp.float32), j...  15.1 us
  transfers between devices with their start and end apart: 7, of which 4 were waited for; matrix products, arithmetic and copies ran while one was open for 5% of the time, Pallas kernels for 0%

commit v1 on v0

v1 whole, which is shorter than its diff:
```python
import functools

import jax
import jax.numpy as jnp
from jax import lax
from jax.experimental import pallas as pl
from jax.experimental.pallas import tpu as pltpu
from jax.sharding import PartitionSpec as P

MESH = pl.DeviceIdType.MESH
F32 = jnp.float32
BF16 = jnp.bfloat16

NX, NZ, NY = 4, 8, 4
NQ = 2 * NY

TOK = 192
TOK2 = 2 * TOK
FEAT = 3072
HALF = FEAT // 2
COLS = 256
ROWS = 384
RANK = 32
CUT = 192

NT = (((1,), (1,)), ((), ()))
TN = (((0,), (0,)), ((), ()))
NN = (((1,), (0,)), ((), ()))


def dot(a, b, dims=NN):
    return lax.dot_general(a, b, dims, preferred_element_type=F32)


def pieces(value, count):
    out = []
    for _ in range(count):
        part = value.astype(BF16)
        out.append(part)
        value = value - part.astype(F32)
    return out


def total(ref, count):
    value = ref[0]
    for i in range(1, count):
        value = value + ref[i]
    return value


def kernel(
    acts, cot, base, at, b, mag,
    gx_out, ga_out, gb_out, gm_out,
    w, actsf, gf, scaled, bf, ah,
    sqx, sqz, ns, tbp, tbi, ctp, cti, ctx, ctz, ctc,
    tpp, tpi, tps, tpzi, tpg, tpf, mox, moz, moq, gaf, gxb, lowo, momt,
    ssem, rsem,
):
    p = lax.axis_index("dp")
    f = lax.axis_index("fsdp")
    y = lax.axis_index("col")
    x = lax.rem(f, NX)
    z = lax.div(f, NX)
    q = 2 * y + p

    def at_xz(nx, nz):
        return (p, nz * NX + nx, y)

    def at_q(nq):
        return (lax.rem(nq, 2), f, lax.div(nq, 2))

    xpeer = lambda d: at_xz(lax.rem(x + d, NX), z)
    zpeer = lambda d: at_xz(x, lax.rem(z + d, NZ))
    qpeer = lambda d: at_q(lax.rem(q + d, NQ))
    ypeer = lambda d: (p, f, lax.rem(y + d, NY))
    core = (1 - p, f, y)
    swap = (lax.rem(z, 2), q * NX + x, lax.div(z, 2))
    fixed = z == q

    n_sem = [0]
    finals = []

    def sems(n):
        n_sem[0] += n
        assert n_sem[0] <= SEMS
        return n_sem[0] - n

    def copy(src, dst, sem, dev):
        return pltpu.make_async_remote_copy(
            src_ref=src, dst_ref=dst, send_sem=ssem.at[sem], recv_sem=rsem.at[sem],
            device_id=dev, device_id_type=MESH,
        )

    def each(lo, hi, body):
        def step(i, carry):
            body(i)
            return carry

        lax.fori_loop(lo, hi, step, 0)

    class Ring:
        def __init__(self, n, me, peer, dst):
            self.n, self.me, self.peer, self.dst = n, me, peer, dst
            self.sem = sems(n)

        def start(self, src):
            def mk(d):
                return copy(src(lax.rem(self.me + d, self.n)), self.dst.at[self.me], self.sem + d, self.peer(d))

            each(1, self.n, lambda d: mk(d).start())
            finals.append(lambda: each(1, self.n, lambda d: mk(d).wait_send()))

        def wait(self):
            def one(d):
                here = self.dst.at[lax.rem(self.me - d + self.n, self.n)]
                copy(here, here, self.sem + d, self.peer(d)).wait_recv()

            each(1, self.n, one)

    bar = pltpu.get_barrier_semaphore()
    each(1, NX, lambda d: pl.semaphore_signal(bar, inc=1, device_id=xpeer(d), device_id_type=MESH))
    each(1, NZ, lambda d: pl.semaphore_signal(bar, inc=1, device_id=zpeer(d), device_id_type=MESH))
    each(1, NQ, lambda d: pl.semaphore_signal(bar, inc=1, device_id=qpeer(d), device_id_type=MESH))

    @pl.when(jnp.logical_not(fixed))
    def _():
        pl.semaphore_signal(bar, inc=1, device_id=swap, device_id_type=MESH)
        pl.semaphore_wait(bar, NX + NZ + NQ - 2)

    @pl.when(fixed)
    def _():
        pl.semaphore_wait(bar, NX + NZ + NQ - 3)

    PARTS = ((0, CUT), (CUT, ROWS))
    s_swap = sems(2)

    def swap_copy(i):
        lo, hi = PARTS[i]
        return copy(base.at[p, pl.ds(lo, hi - lo), :], w.at[q, x, pl.ds(lo, hi - lo), :], s_swap + i, swap)

    @pl.when(jnp.logical_not(fixed))
    def _():
        swap_copy(1).start()
        swap_copy(0).start()

    def wait_swap(i):
        lo, hi = PARTS[i]
        here = w.at[z, x, pl.ds(lo, hi - lo), :]

        @pl.when(jnp.logical_not(fixed))
        def _():
            copy(here, here, s_swap + i, swap).wait_recv()

        @pl.when(fixed)
        def _():
            w[z, x, lo:hi, :] = base[p, lo:hi, :]

    def final_swap():
        @pl.when(jnp.logical_not(fixed))
        def _():
            swap_copy(0).wait_send()
            swap_copy(1).wait_send()

    finals.append(final_swap)

    s_acts = sems(1)
    mine = pl.ds(pl.multiple_of(p * TOK, TOK), TOK)
    others = pl.ds(pl.multiple_of((1 - p) * TOK, TOK), TOK)
    my_half = pl.ds(pl.multiple_of(p * HALF, HALF), HALF)
    other_half = pl.ds(pl.multiple_of((1 - p) * HALF, HALF), HALF)
    acts_copy = copy(acts.at[:, other_half], actsf.at[mine, :], s_acts, core)
    acts_copy.start()
    finals.append(acts_copy.wait_send)

    s_goty, s_gotc = sems(2 * NY), sems(2 * NY)

    def cot_y(d, k):
        return copy(cot.at[k], gf.at[2 * y + k, mine, :], s_goty + 2 * d + k, ypeer(d))

    def cot_c(d, k, src=None):
        there = gf.at[2 * lax.rem(y - d + NY, NY) + k, mine, :]
        return copy(there if src is None else src, there, s_gotc + 2 * d + k, core)

    def cot_start(d):
        for k in range(2):
            cot_y(d, k).start()

    each(1, NY, cot_start)
    for k in range(2):
        cot_c(0, k, cot.at[k]).start()
    finals.append(lambda: [cot_c(0, k, cot.at[k]).wait_send() for k in range(2)])

    def cot_final(d):
        for k in range(2):
            cot_y(d, k).wait_send()
            cot_c(d, k).wait_send()

    finals.append(lambda: each(1, NY, cot_final))

    def cot_relay():
        def one(d):
            for k in range(2):
                here = gf.at[2 * lax.rem(y - d + NY, NY) + k, mine, :]
                copy(here, here, s_goty + 2 * d + k, core).wait_recv()
                cot_c(d, k).start()

        each(1, NY, one)

    def cot_wait():
        def one(d):
            for k in range(2):
                here = gf.at[2 * lax.rem(y - d + NY, NY) + k, others, :]
                copy(here, here, s_gotc + 2 * d + k, core).wait_recv()

        each(0, NY, one)

    r_b = Ring(NY, y, ypeer, bf)
    r_b.start(lambda _: b)
    bf[y] = b[...]

    s_ax, s_az, s_bz, s_bx = sems(NX), sems(NX * 8), sems(8), sems(9 * NX)

    def ring_rows(part, way, s):
        lo, hi = PARTS[part]
        if s < 3:
            return lo, hi - lo
        half = (hi - lo) // 2
        return lo + way * half, half

    def origin(way, s):
        return lax.rem(z - s + NZ, NZ) if way == 0 else lax.rem(z + s, NZ)

    def z_copy(part, j, way, s):
        lo, n = ring_rows(part, way, s)
        here = w.at[origin(way, s), lax.rem(x - j + NX, NX), pl.ds(lo, n), :]
        sem = (s_az + (j * 2 + way) * 4 + s) if part == 0 else (s_bz + way * 4 + s)
        return copy(here, here, sem, zpeer(1 if way == 0 else NZ - 1))

    def z_arrival(part, j, way, s):
        lo, n = ring_rows(part, way, s)
        here = w.at[origin(way, s + 1), lax.rem(x - j + NX, NX), pl.ds(lo, n), :]
        sem = (s_az + (j * 2 + way) * 4 + s) if part == 0 else (s_bz + way * 4 + s)
        copy(here, here, sem, zpeer(1)).wait_recv()

    def z_start(part, j, way, s):
        z_copy(part, j, way, s).start()
        finals.append(lambda: z_copy(part, j, way, s).wait_send())

    def bx_copy(d, way, s):
        lo, n = ring_rows(1, way, s - 1)
        here = w.at[origin(way, s), x, pl.ds(lo, n), :]
        slot = 0 if s == 0 else 1 + way * 4 + s - 1
        return copy(here, here, s_bx + slot * NX + d, xpeer(d))

    def bx_start(way, s):
        each(1, NX, lambda d: bx_copy(d, way, s).start())
        finals.append(lambda: each(1, NX, lambda d: bx_copy(d, way, s).wait_send()))

    def bx_wait(way, s):
        lo, n = ring_rows(1, way, s - 1)
        slot = 0 if s == 0 else 1 + way * 4 + s - 1

        def one(d):
            here = w.at[origin(way, s), lax.rem(x - d + NX, NX), pl.ds(lo, n), :]
            copy(here, here, s_bx + slot * NX + d, xpeer(d)).wait_recv()

        each(1, NX, one)

    def ax_copy(d):
        here = w.at[z, x, pl.ds(0, CUT), :]
        return copy(here, here, s_ax + d, xpeer(d))

    def ax_wait(d):
        here = w.at[z, lax.rem(x - d + NX, NX), pl.ds(0, CUT), :]
        copy(here, here, s_ax + d, xpeer(d)).wait_recv()

    r_sqx = Ring(NX, x, xpeer, sqx)
    r_sqz = Ring(NZ, z, zpeer, sqz)
    r_ns = Ring(NQ, q, qpeer, ns)
    a_rows = at[p, :, pl.ds(pl.multiple_of(f * ROWS, ROWS), ROWS)]
    composed = base[p].astype(F32) + dot(a_rows, b[p], TN)
    sqx[x] = jnp.broadcast_to(jnp.sum(composed * composed, axis=0, keepdims=True), (8, COLS))
    r_sqx.start(lambda _: sqx.at[x])
    across = functools.reduce(lambda u, v: u + v, [dot(a_rows, c) for c in pieces(composed, 3)])

    wait_swap(1)
    for way in range(2):
        z_start(1, 0, way, 0)
    wait_swap(0)
    each(1, NX, lambda d: ax_copy(d).start())
    finals.append(lambda: each(1, NX, lambda d: ax_copy(d).wait_send()))
    for way in range(2):
        z_start(0, 0, way, 0)
    bx_start(0, 0)

    ah[0:RANK] = at[0, :, pl.ds(pl.multiple_of(q * HALF, HALF), HALF)]
    ah[RANK:] = at[1, :, pl.ds(pl.multiple_of(q * HALF, HALF), HALF)]
    actsf[mine, :] = acts[:, my_half]
    for k in range(2):
        gf[2 * y + k, mine, :] = cot[k]

    r_sqx.wait()
    sqz[z] = total(sqx, NX)
    r_sqz.start(lambda _: sqz.at[z])

    for j in range(1, NX):
        ax_wait(j)
        for way in range(2):
            z_start(0, j, way, 0)

    here_acts = actsf.at[others, :]
    copy(here_acts, here_acts, s_acts, core).wait_recv()
    low_in = dot(ah[...], actsf[...], NT)

    r_sqz.wait()
    norms = jnp.sqrt(total(sqz, NZ)[0:1])
    ns[q, 0:1] = norms
    ns[q, 1:2] = mag[pl.ds(p, 1), :] / norms
    r_ns.start(lambda _: ns.at[q])
    cot_relay()

    def ring_b(s):
        for way in range(2):
            z_arrival(1, 0, way, s - 1)
            if s < 4:
                z_start(1, 0, way, s)
            bx_start(way, s)

    def ring_a(s):
        for j in range(NX):
            for way in range(2):
                z_arrival(0, j, way, s - 1)
                if s < 4:
                    z_start(0, j, way, s)

    def forward(zi):
        out = dot(actsf[...], w[zi].reshape(NX * ROWS, COLS))
        momt[pl.ds(zi, 1), :] = jnp.sum(out * gf[zi].astype(F32), axis=0, keepdims=True)

    ring_b(1)
    r_b.wait()
    cot_wait()

    r_tb = Ring(NQ, q, qpeer, tbi)
    for k in range(2):
        parts = jnp.concatenate(pieces(low_in[k * RANK : (k + 1) * RANK], 3), axis=0)
        for yy in range(NY):
            t = dot(parts, gf[2 * yy + k])
            tbp[2 * yy + k] = t[0:RANK] + t[RANK : 2 * RANK] + t[2 * RANK :]
    tbi[q] = tbp[q]
    r_tb.start(lambda i: tbp.at[i])

    ring_a(1)

    r_ns.wait()
    low = []
    for k in range(2):
        acc = None
        for yy in range(NY):
            i = 2 * yy + k
            s = (gf[i].astype(F32) * ns[i, 1:2]).astype(BF16)
            scaled[i] = s
            t = dot(s, bf[yy, k], NT)
            acc = t if acc is None else acc + t
        low.append(acc)
    lowf = jnp.concatenate(low, axis=1)
    lowo[...] = lowf.astype(BF16)
    lowt = lowf.T.astype(BF16)
    r_tpx = Ring(NX, x, xpeer, tpi)
    for xx in range(NX):
        tpp[xx] = dot(lowt, actsf[:, xx * ROWS : (xx + 1) * ROWS])
    tpi[x] = tpp[x]
    r_tpx.start(lambda i: tpp.at[i])

    ring_b(2)

    bx_wait(0, 0)
    forward(z)
    for way in range(2):
        bx_wait(way, 1)
        forward(origin(way, 1))

    r_tb.wait()
    token_b = total(tbi, NQ)
    r_ctz = Ring(NZ, z, zpeer, cti)
    r_ctx = Ring(NX, x, xpeer, ctx)
    r_ctg = Ring(NZ, z, zpeer, ctz)
    for g in range(NZ):
        ctp[g, 0:4] = across[4 * g : 4 * g + 4]
        ctp[g, 4:8] = token_b[4 * g : 4 * g + 4]
    cti[z] = ctp[z]
    r_ctz.start(lambda i: ctp.at[i])

    ring_a(2)

    r_tpz = Ring(NZ, z, zpeer, tpzi)
    r_tpg = Ring(NZ, z, zpeer, tpg)
    r_tpf = Ring(NX, x, xpeer, tpf)
    r_tpx.wait()
    tps[...] = total(tpi, NX).reshape(NZ, 8, ROWS)
    tpzi[z] = tps[z]
    r_tpz.start(lambda i: tps.at[i])

    ring_b(3)

    for way in range(2):
        bx_wait(way, 2)
        forward(origin(way, 2))

    r_ctz.wait()
    ctx[x] = total(cti, NZ)
    r_ctx.start(lambda _: ctx.at[x])
    r_tpz.wait()
    tpg[z] = total(tpzi, NZ)
    r_tpg.start(lambda _: tpg.at[z])

    ring_a(3)

    r_ctx.wait()
    ctz[z] = total(ctx, NX)
    r_ctg.start(lambda _: ctz.at[z])
    r_tpg.wait()
    tpf[x] = tpg[...]
    r_tpf.start(lambda _: tpg)

    ring_b(4)

    for way in range(2):
        bx_wait(way, 3)
        forward(origin(way, 3))

    r_ctg.wait()
    ctc[p] = ctz[...]
    s_ctc = sems(1)
    ctc_copy = copy(ctz, ctc.at[p], s_ctc, core)
    ctc_copy.start()
    finals.append(ctc_copy.wait_send)

    ring_a(4)

    for way in range(2):
        bx_wait(way, 4)
    forward(origin(0, 4))

    r_mox = Ring(NX, x, xpeer, mox)
    r_moz = Ring(NZ, z, zpeer, moz)
    r_moq = Ring(NQ, q, qpeer, moq)
    extra = []
    for i in range(NQ):
        extra.append(jnp.sum(tbp[i] * bf[i // 2, i % 2].astype(F32), axis=0, keepdims=True))
    mox[x] = momt[...] + jnp.concatenate(extra, axis=0)
    r_mox.start(lambda _: mox.at[x])

    def backward(xx):
        acc = dot(lowo[...], ah[:, xx * ROWS : (xx + 1) * ROWS])
        for zi in range(NZ):
            acc = acc + dot(scaled[zi], w[zi, xx], NT)
        gxb[:, xx * ROWS : (xx + 1) * ROWS] = acc.astype(BF16)

    backward(0)
    r_mox.wait()
    moz[z] = total(mox, NX)
    r_moz.start(lambda _: moz.at[z])
    backward(1)
    backward(2)
    r_moz.wait()
    moq[q] = total(moz, NZ)
    r_moq.start(lambda _: moq.at[q])
    backward(3)

    s_gx = sems(1)
    gx_copy = copy(gxb.at[others, :], gx_out.at[:, my_half], s_gx, core)
    gx_copy.start()
    finals.append(gx_copy.wait_send)
    gx_out[:, my_half] = gxb[mine, :]

    r_moq.wait()
    moment = total(moq, NQ)
    norm_all = jnp.concatenate([ns[i, 0:1] for i in range(NQ)], axis=0)
    scal_all = jnp.concatenate([ns[i, 1:2] for i in range(NQ)], axis=0)
    grad_mag = moment / norm_all
    factor = scal_all * grad_mag / norm_all
    momt[...] = grad_mag

    r_tpf.wait()
    for k in range(2):
        weights = []
        inner = None
        for yy in range(NY):
            i = 2 * yy + k
            two = jnp.concatenate(pieces(bf[yy, k].astype(F32) * factor[i : i + 1], 2), axis=0)
            weights.append(two)
            t = dot(two, bf[yy, k], NT)
            inner = t if inner is None else inner + t
        inner = jnp.concatenate(pieces(inner[0:RANK] + inner[RANK:], 2), axis=0)
        for xx in range(NX):
            span = slice(xx * ROWS, (xx + 1) * ROWS)
            acc = dot(inner, ah[k * RANK : (k + 1) * RANK, span])
            for yy in range(NY):
                acc = acc + dot(weights[yy], w[2 * yy + k, xx], NT)
            tokens = tpf[xx].reshape(2 * RANK, ROWS)[k * RANK : (k + 1) * RANK]
            gaf[q, k * RANK : (k + 1) * RANK, span] = (tokens - (acc[0:RANK] + acc[RANK:])).astype(BF16)

    s_gay, s_gac = sems(NY), sems(NY)

    def ga_y(d):
        return copy(gaf.at[q], gaf.at[q], s_gay + d, ypeer(d))

    def ga_c(d):
        here = gaf.at[2 * lax.rem(y - d + NY, NY) + p]
        return copy(here, here, s_gac + d, core)

    each(1, NY, lambda d: ga_y(d).start())
    ga_c(0).start()

    copy(ctc.at[1 - p], ctc.at[1 - p], s_ctc, core).wait_recv()
    for k in range(2):
        i = 2 * y + k
        norm_k = ns[i, 0:1]
        scal_k = ns[i, 1:2]
        gm_k = momt[pl.ds(i, 1), :]
        gm_out[k : k + 1] = gm_k
        ratio = gm_k / norm_k
        for g in range(NZ):
            gb_out[k, 4 * g : 4 * g + 4] = scal_k * (ctc[k, g, 4:8] - ctc[k, g, 0:4] * ratio)

    def ga_relay(d):
        here = gaf.at[2 * lax.rem(y - d + NY, NY) + p]
        copy(here, here, s_gay + d, core).wait_recv()
        ga_c(d).start()

    each(1, NY, ga_relay)

    def ga_wait(d):
        here = gaf.at[2 * lax.rem(y - d + NY, NY) + 1 - p]
        copy(here, here, s_gac + d, core).wait_recv()

    each(0, NY, ga_wait)
    for i in range(NQ):
        for k in range(2):
            ga_out[k, :, i * HALF : (i + 1) * HALF] = gaf[i, k * RANK : (k + 1) * RANK]

    def ga_final(d):
        ga_y(d).wait_send()
        ga_c(d).wait_send()

    each(1, NY, ga_final)
    ga_c(0).wait_send()
    here_gx = gx_out.at[:, other_half]
    copy(here_gx, here_gx, s_gx, core).wait_recv()
    for final in finals:
        final()


SEMS = 256


def on_device(acts, cot, base, adapter_a, adapter_b, magnitude):
    at = jnp.swapaxes(adapter_a, 1, 2)
    vm = pl.BlockSpec(memory_space=pltpu.VMEM)
    scratch = [
        ((NZ, NX, ROWS, COLS), BF16),
        ((TOK2, HALF), BF16),
        ((NQ, TOK2, COLS), BF16),
        ((NQ, TOK2, COLS), BF16),
        ((NY, 2, RANK, COLS), BF16),
        ((2 * RANK, HALF), BF16),
        ((NX, 8, COLS), F32),
        ((NZ, 8, COLS), F32),
        ((NQ, 8, COLS), F32),
        ((NQ, RANK, COLS), F32),
        ((NQ, RANK, COLS), F32),
        ((NZ, 8, COLS), F32),
        ((NZ, 8, COLS), F32),
        ((NX, 8, COLS), F32),
        ((NZ, 8, COLS), F32),
        ((2, NZ, 8, COLS), F32),
        ((NX, 2 * RANK, ROWS), F32),
        ((NX, 2 * RANK, ROWS), F32),
        ((NZ, 8, ROWS), F32),
        ((NZ, 8, ROWS), F32),
        ((NZ, 8, ROWS), F32),
        ((NX, NZ, 8, ROWS), F32),
        ((NX, 8, COLS), F32),
        ((NZ, 8, COLS), F32),
        ((NQ, 8, COLS), F32),
        ((NQ, 2 * RANK, HALF), BF16),
        ((TOK2, HALF), BF16),
        ((TOK2, 2 * RANK), BF16),
        ((NQ, COLS), F32),
    ]
    gx, ga, gb, gm = pl.pallas_call(
        kernel,
        out_shape=(
            jax.ShapeDtypeStruct((TOK, FEAT), BF16),
            jax.ShapeDtypeStruct((2, RANK, NQ * HALF), BF16),
            jax.ShapeDtypeStruct((2, RANK, COLS), F32),
            jax.ShapeDtypeStruct((2, COLS), F32),
        ),
        in_specs=[vm] * 6,
        out_specs=(vm,) * 4,
        scratch_shapes=[pltpu.VMEM(shape, dtype) for shape, dtype in scratch]
        + [pltpu.SemaphoreType.DMA((SEMS,)), pltpu.SemaphoreType.DMA((SEMS,))],
        compiler_params=pltpu.CompilerParams(
            collective_id=0, has_side_effects=True, vmem_limit_bytes=56 * 2**20
        ),
        cost_estimate=pl.CostEstimate(flops=5 * 10**9, bytes_accessed=8 * 10**6, transcendentals=0),
    )(acts, cot, base, at, adapter_b, magnitude)
    return gx, jnp.swapaxes(ga.astype(F32), 1, 2), gb, gm


def solution(mesh):
    in_specs = (
        P(("dp", "fsdp"), "col"),
        P(None, ("dp", "fsdp"), "col"),
        P(None, "fsdp", "col"),
        P(),
        P(None, None, "col"),
        P(None, "col"),
    )
    out_specs = (P(("dp", "fsdp"), "col"), P(), P(None, None, "col"), P(None, "col"))
    return jax.shard_map(
        on_device, mesh=mesh, in_specs=in_specs, out_specs=out_specs, check_vma=False
    )
```

time: 743 us -> 124 us (0.17)
  waiting for transfers between devices: 646 us -> 0 us
  Pallas kernels: 0 us -> 118 us
  matrix products: 45.2 us -> 0 us
  blocking collectives: 15.1 us -> 0 us
  between operations: 15.7 us -> 0.65 us
  local copies, waits for them, and re-layouts: 9.77 us -> 2.23 us
    psum x3 -> x0, waiting for transfers between devices: 586 us -> none  [the longest x1 275 us: on_device(): list_a.append(lax.psum(adapter_term, ('dp', 'fsdp', 'col')))]
    pallas_call x0 -> x1, Pallas kernels: none -> 118 us  [on_device(): pl.pallas_call(kernel, out_shape=(jax.ShapeDtypeStruct((TOK, FEAT), BF16)...]
    all_gather x3 -> x0, waiting for transfers between devices: 58.9 us -> none  [the longest x2 58.9 us: on_device(): piece = lax.all_gather(base[which], 'fsdp', axis=0, tiled=True)]
    dot_general x22 -> x0, matrix products: 45.2 us -> none  [the longest x2 13.8 us: on_device(): jnp.einsum('tj,ij->ti', scaled, piece, preferred_element_type=jnp.float32)]
    psum x1 -> x0, blocking collectives: 15.1 us -> none  [on_device(): lax.psum((jnp.dot(acts, down_cols, preferred_element_type=jnp.float32), j...]
  transfers between devices with their start and end apart: 7 -> 0, of which waited for: 4 -> 0; matrix products, arithmetic and copies ran while one was open for 5% -> 0% of each run, Pallas kernels for 0% -> 0%
where the time goes in v1:
time: 124 us
  Pallas kernels  118 us (95%)
  other arithmetic  3.37 us (3%)
  local copies, waits for them, and re-layouts  2.23 us (2%)
    pallas_call x1, Pallas kernels, on_device(): pl.pallas_call(kernel, out_shape=(jax.ShapeDtypeStruct((TOK, FEAT), BF16)...  118 us
    transpose x1, other arithmetic, on_device(): return (gx, jnp.swapaxes(ga.astype(F32), 1, 2), gb, gm)  3.37 us

profile of v1, /device:TPU:1, one launch (start us, length us, event | category | flops | bytes accessed | tf_op | source)
XLA Modules:
  0.0 124.0 jit_solution(6448985553802495394)
XLA Ops:
  0.6 117.7 %shard_map.93 = (bf16[192,3072]{1,0:T(8,128)(2,1)}, bf16[2,32,12288]{2,1,0:T(8,128)(2,1)}, f32[2,32,256]{2,1,0:T(8,128)}, f32[2,256]{1,0:T(2,128)}) custom-call(bf16[192,3072]{1,0:T(8,128)(2,1)} %acts.1, bf16[2,192,256]{2,1,0:T(8,128)(2,1)} %cot.1, bf16[2,384,256]{2,1,0:T(8,128)(2,1)} %base.1, bf16[2,32,12288]{2,1,0:T(8,128)(2,1)} %bitcast.3, ...), custom_call_target="tpu_custom_call" | custom-call | flops 5000000000 | bytes 8000000 | tf_op jit(solution)/shard_map/pallas_call | solution.py:592
  118.3 0.0 copy-start
  118.4 3.4 %convert_bitcast_fusion = f32[2,12288,32]{1,2,0:T(8,128)} fusion(bf16[2,32,12288]{2,1,0:T(8,128)(2,1)} %get-tuple-element.9), kind=kLoop, calls=%fused_computation | loop fusion | flops 786432 | bytes 4718592 | tf_op jit(solution)/shard_map/transpose | solution.py:609
  121.7 0.0 copy-done
  121.7 0.0 copy-start.1
  121.7 0.0 copy-start.2
  121.7 1.0 copy.13
  122.7 0.0 copy-done.1
  122.7 0.6 copy.14
  123.4 0.0 copy-done.2
  123.4 0.6 copy.15
Async XLA Ops:
  118.3 3.4 %copy-start = (bf16[192,3072]{1,0:T(8,128)(2,1)S(1)}, bf16[192,3072]{1,0:T(8,128)(2,1)}, u32[]{:S(2)}) copy-start(bf16[192,3072]{1,0:T(8,128)(2,1)} %get-tuple-element.16) | copy-start | bytes 3538948
  121.7 1.0 copy-start.1
  121.7 1.7 %copy-start.2 = (f32[2,256]{1,0:T(2,128)S(1)}, f32[2,256]{1,0:T(2,128)}, u32[]{:S(2)}) copy-start(f32[2,256]{1,0:T(2,128)} %get-tuple-element.19) | copy-start | bytes 6148

commit v2 on v1

v2 whole, which is shorter than its diff:
```python
import functools

import jax
import jax.numpy as jnp
from jax import lax
from jax.experimental import pallas as pl
from jax.experimental.pallas import tpu as pltpu
from jax.sharding import PartitionSpec as P

MESH = pl.DeviceIdType.MESH
F32 = jnp.float32
BF16 = jnp.bfloat16

NX, NZ, NY = 4, 8, 4
NQ = 2 * NY

TOK = 192
TOK2 = 2 * TOK
FEAT = 3072
HALF = FEAT // 2
COLS = 256
ROWS = 384
RANK = 32
CUT = 160

NT = (((1,), (1,)), ((), ()))
TN = (((0,), (0,)), ((), ()))
NN = (((1,), (0,)), ((), ()))


def dot(a, b, dims=NN):
    return lax.dot_general(a, b, dims, preferred_element_type=F32)


def pieces(value, count):
    out = []
    for _ in range(count):
        part = value.astype(BF16)
        out.append(part)
        value = value - part.astype(F32)
    return out


def total(ref, count):
    value = ref[0]
    for i in range(1, count):
        value = value + ref[i]
    return value


def kernel(
    acts, cot, base, at, b, mag,
    gx_out, ga_out, gb_out, gm_out,
    w, actsf, gf, scaled, bf, ah, ar, mybase,
    sqx, sqz, ns, tbp, tbi, ctp, cti, ctx, ctz, ctc,
    tpp, tpi, tps, tpzi, tpg, mox, moz, moq, gaf, gxb, lowo, momt, wts, inr,
    ssem, rsem, lsem,
):
    p = lax.axis_index("dp")
    f = lax.axis_index("fsdp")
    y = lax.axis_index("col")
    x = lax.rem(f, NX)
    z = lax.div(f, NX)
    q = 2 * y + p

    def at_xz(nx, nz):
        return (p, nz * NX + nx, y)

    def at_q(nq):
        return (lax.rem(nq, 2), f, lax.div(nq, 2))

    xpeer = lambda d: at_xz(lax.rem(x + d, NX), z)
    zpeer = lambda d: at_xz(x, lax.rem(z + d, NZ))
    qpeer = lambda d: at_q(lax.rem(q + d, NQ))
    ypeer = lambda d: (p, f, lax.rem(y + d, NY))
    core = (1 - p, f, y)

    def shift(c):
        k, half = lax.rem(c, 2), lax.div(c, 2)
        return lax.rem((1 - k) * half + k * (4 + (4 - half) * jnp.minimum(half, 1)), NZ)

    def chunk_at(position):
        step = lax.rem(position - q + NZ, NZ)
        far = lax.div(step, 4)
        return (1 - far) * 2 * step + far * lax.rem(17 - 2 * step, NZ)

    target = (lax.rem(z, 2), lax.rem(z + shift(q), NZ) * NX + x, lax.div(z, 2))
    own = chunk_at(z)
    source = (lax.rem(own, 2), q * NX + x, lax.div(own, 2))
    fixed = jnp.logical_and(own == q, z == q)

    counts = {"send": 0, "recv": 0, "local": 0}
    limits = {"send": SENDS, "recv": RECVS, "local": LOCALS}
    finals = []

    def sems(kind, n=1):
        counts[kind] += n
        assert counts[kind] <= limits[kind]
        return counts[kind] - n

    def copy(src, dst, send, recv, dev):
        return pltpu.make_async_remote_copy(
            src_ref=src, dst_ref=dst, send_sem=ssem.at[send], recv_sem=rsem.at[recv],
            device_id=dev, device_id_type=MESH,
        )

    def arrived(ref, recv):
        copy(ref, ref, 0, recv, core).wait_recv()

    def sent(ref, send):
        finals.append(lambda: copy(ref, ref, send, 0, core).wait_send())

    def each(lo, hi, body):
        def step(i, carry):
            body(i)
            return carry

        lax.fori_loop(lo, hi, step, 0)

    class Ring:
        def __init__(self, n, me, peer, dst):
            self.n, self.me, self.peer, self.dst = n, me, peer, dst
            self.send, self.recv = sems("send"), sems("recv")

        def start(self, src):
            def one(d):
                block = src(lax.rem(self.me + d, self.n))
                copy(block, self.dst.at[self.me], self.send, self.recv, self.peer(d)).start()

            each(1, self.n, one)
            sent(self.dst.at[pl.ds(0, self.n - 1)], self.send)

        def wait(self):
            arrived(self.dst.at[pl.ds(0, self.n - 1)], self.recv)

    mine = pl.ds(pl.multiple_of(p * TOK, TOK), TOK)
    others = pl.ds(pl.multiple_of((1 - p) * TOK, TOK), TOK)
    my_half = pl.ds(pl.multiple_of(p * HALF, HALF), HALF)
    other_half = pl.ds(pl.multiple_of((1 - p) * HALF, HALF), HALF)

    loads = [
        pltpu.make_async_copy(base.at[p], mybase, lsem.at[sems("local")]),
        pltpu.make_async_copy(at.at[p, :, pl.ds(pl.multiple_of(f * ROWS, ROWS), ROWS)], ar, lsem.at[sems("local")]),
    ]
    for k in range(2):
        rows = pl.ds(k * RANK, RANK)
        span = pl.ds(pl.multiple_of(q * HALF, HALF), HALF)
        loads.append(pltpu.make_async_copy(at.at[k, :, span], ah.at[rows, :], lsem.at[sems("local")]))
        loads.append(pltpu.make_async_copy(cot.at[k], gf.at[2 * y + k, mine, :], lsem.at[sems("local")]))
    loads.append(pltpu.make_async_copy(acts.at[:, my_half], actsf.at[mine, :], lsem.at[sems("local")]))
    for load in loads:
        load.start()

    bar = pltpu.get_barrier_semaphore()
    each(1, NX, lambda d: pl.semaphore_signal(bar, inc=1, device_id=xpeer(d), device_id_type=MESH))
    each(1, NZ, lambda d: pl.semaphore_signal(bar, inc=1, device_id=zpeer(d), device_id_type=MESH))
    each(1, NQ, lambda d: pl.semaphore_signal(bar, inc=1, device_id=qpeer(d), device_id_type=MESH))

    @pl.when(jnp.logical_not(fixed))
    def _():
        pl.semaphore_signal(bar, inc=1, device_id=source, device_id_type=MESH)

    r_sqx = Ring(NX, x, xpeer, sqx)
    r_sqz = Ring(NZ, z, zpeer, sqz)
    r_ns = Ring(NQ, q, qpeer, ns)
    bf[y] = b[...]
    for load in loads:
        load.wait()
    composed = mybase[...].astype(F32) + dot(ar[...], b[p], TN)
    sqx[x] = jnp.broadcast_to(jnp.sum(composed * composed, axis=0, keepdims=True), (8, COLS))
    across = functools.reduce(lambda u, v: u + v, [dot(ar[...], c) for c in pieces(composed, 3)])

    @pl.when(jnp.logical_not(fixed))
    def _():
        pl.semaphore_wait(bar, NX + NZ + NQ - 2)

    @pl.when(fixed)
    def _():
        pl.semaphore_wait(bar, NX + NZ + NQ - 3)

    PARTS = ((0, CUT), (CUT, ROWS))
    s_swap, r_swap = sems("send"), sems("recv", 2)

    def swap_copy(i):
        lo, hi = PARTS[i]
        return copy(mybase.at[pl.ds(lo, hi - lo), :], w.at[q, x, pl.ds(lo, hi - lo), :], s_swap, r_swap + i, target)

    @pl.when(jnp.logical_not(fixed))
    def _():
        swap_copy(1).start()
        swap_copy(0).start()

    def wait_swap(i):
        lo, hi = PARTS[i]

        @pl.when(jnp.logical_not(fixed))
        def _():
            arrived(w.at[own, x, pl.ds(lo, hi - lo), :], r_swap + i)

        @pl.when(fixed)
        def _():
            w[own, x, lo:hi, :] = mybase[lo:hi, :]

    def final_swap():
        @pl.when(jnp.logical_not(fixed))
        def _():
            copy(mybase, mybase, s_swap, 0, target).wait_send()

    finals.append(final_swap)
    r_sqx.start(lambda _: sqx.at[x])

    s_acts, r_acts = sems("send"), sems("recv")
    copy(acts.at[:, other_half], actsf.at[mine, :], s_acts, r_acts, core).start()
    sent(actsf.at[mine, :], s_acts)

    s_goty, s_gotc, r_goty, r_gotc = sems("send"), sems("send"), sems("recv", NY), sems("recv")

    def cot_core(d):
        for k in range(2):
            here = gf.at[2 * lax.rem(y - d + NY, NY) + k, mine, :]
            copy(here, here, s_gotc, r_gotc, core).start()

    def cot_start():
        def one(d):
            for k in range(2):
                here = gf.at[2 * y + k, mine, :]
                copy(here, here, s_goty, r_goty + d, ypeer(d)).start()

        each(1, NY, one)
        cot_core(0)
        sent(gf.at[pl.ds(0, NY - 1)], s_goty)
        sent(gf.at[pl.ds(0, NY)], s_gotc)

    def cot_relay():
        def one(d):
            arrived(gf.at[0], r_goty + d)
            cot_core(d)

        each(1, NY, one)

    def cot_wait():
        arrived(gf.at[pl.ds(0, NY)], r_gotc)

    r_b = Ring(NY, y, ypeer, bf)
    r_b.start(lambda i: bf.at[y])

    s_ax, s_az, s_bz, s_bx = sems("send"), sems("send"), sems("send"), sems("send")
    r_ax, r_az, r_bz = sems("recv", NX), sems("recv", NX * 8), sems("recv", 8)
    r_bx, r_bx4 = sems("recv", 7 * 3), sems("recv")
    b_lo, b_n = CUT, ROWS - CUT
    b_half = b_n // 2

    def ring_rows(part, way, s):
        lo, hi = PARTS[part]
        if s < 3:
            return lo, hi - lo
        half = (hi - lo) // 2
        return lo + way * half, half

    def origin(way, s):
        return chunk_at(lax.rem(z - s + NZ, NZ) if way == 0 else lax.rem(z + s, NZ))

    def z_sem(part, j, way, s):
        return (r_az + (j * 2 + way) * 4 + s) if part == 0 else (r_bz + way * 4 + s)

    def z_start(part, j, way, s):
        lo, n = ring_rows(part, way, s)
        here = w.at[origin(way, s), lax.rem(x - j + NX, NX), pl.ds(lo, n), :]
        send = s_az if part == 0 else s_bz
        copy(here, here, send, z_sem(part, j, way, s), zpeer(1 if way == 0 else NZ - 1)).start()

    def z_arrival(part, j, way, s):
        lo, n = ring_rows(part, way, s)
        arrived(w.at[origin(way, s + 1), lax.rem(x - j + NX, NX), pl.ds(lo, n), :], z_sem(part, j, way, s))

    sent(w.at[pl.ds(0, 7), :, pl.ds(0, CUT), :], s_az)
    sent(w.at[pl.ds(0, 7), 0, pl.ds(b_lo, b_n), :], s_bz)
    sent(w.at[pl.ds(0, 6), :, pl.ds(b_lo, b_n), :], s_bx)
    sent(w.at[0, pl.ds(0, 3), pl.ds(0, CUT), :], s_ax)

    def bx_sem(way, s):
        return r_bx + 3 * (0 if s == 0 else 1 + way * 3 + s - 1)

    def bx_start(way, s):
        here = w.at[origin(way, s), x, pl.ds(b_lo, b_n), :]
        for turn in range(2):
            copy(here, here, s_bx, bx_sem(way, s) + turn, xpeer(1 if turn == 0 else NX - 1)).start()

    def bx_forward(way, s):
        for turn in range(2):
            block = w.at[origin(way, s), lax.rem(x + (NX - 1 if turn == 0 else 1), NX)]
            arrived(block.at[pl.ds(b_lo, b_n), :], bx_sem(way, s) + turn)
            here = block.at[pl.ds(b_lo + turn * b_half, b_half), :]
            copy(here, here, s_bx, bx_sem(way, s) + 2, xpeer(1 if turn == 0 else NX - 1)).start()

    def bx_wait(way, s):
        arrived(w.at[origin(way, s), lax.rem(x + 2, NX), pl.ds(b_lo, b_n), :], bx_sem(way, s) + 2)

    def bx4_start(way):
        here = w.at[origin(way, 4), x, pl.ds(b_lo + way * b_half, b_half), :]
        each(1, NX, lambda d: copy(here, here, s_bx, r_bx4, xpeer(d)).start())

    def bx4_wait():
        arrived(w.at[0, pl.ds(0, 3), pl.ds(b_lo, b_n), :], r_bx4)

    r_sqx.wait()
    sqz[z] = total(sqx, NX)
    r_sqz.start(lambda _: sqz.at[z])
    wait_swap(1)
    for way in range(2):
        z_start(1, 0, way, 0)
    wait_swap(0)
    here_a = w.at[own, x, pl.ds(0, CUT), :]
    each(1, NX, lambda d: copy(here_a, here_a, s_ax, r_ax + d, xpeer(d)).start())
    for way in range(2):
        z_start(0, 0, way, 0)
    bx_start(0, 0)
    cot_start()
    arrived(actsf.at[others, :], r_acts)
    low_in = dot(ah[...], actsf[...], NT)
    r_sqz.wait()
    norms = jnp.sqrt(total(sqz, NZ)[0:1])
    ns[q, 0:1] = norms
    ns[q, 1:2] = mag[pl.ds(p, 1), :] / norms
    r_ns.start(lambda _: ns.at[q])
    for j in range(1, NX):
        arrived(w.at[own, lax.rem(x - j + NX, NX), pl.ds(0, CUT), :], r_ax + j)
        for way in range(2):
            z_start(0, j, way, 0)

    def ring_b(s):
        for way in range(2):
            z_arrival(1, 0, way, s - 1)
            if s < 4:
                z_start(1, 0, way, s)
                bx_start(way, s)
            else:
                bx4_start(way)

    def ring_a(s, *between):
        for j in range(NX):
            for way in range(2):
                z_arrival(0, j, way, s - 1)
                if s < 4:
                    z_start(0, j, way, s)
            if j < len(between):
                between[j]()

    def forward(zi):
        out = dot(actsf[...], w[zi].reshape(NX * ROWS, COLS))
        momt[pl.ds(zi, 1), :] = jnp.sum(out * gf[zi].astype(F32), axis=0, keepdims=True)

    r_tb = Ring(NQ, q, qpeer, tbi)
    r_ctz = Ring(NZ, z, zpeer, cti)
    r_ctx = Ring(NX, x, xpeer, ctx)
    r_ctg = Ring(NZ, z, zpeer, ctz)
    r_tpx = Ring(NX, x, xpeer, tpi)
    r_tpz = Ring(NZ, z, zpeer, tpzi)
    r_tpg = Ring(NZ, z, zpeer, tpg)

    def send_token_b():
        for k in range(2):
            parts = jnp.concatenate(pieces(low_in[k * RANK : (k + 1) * RANK], 3), axis=0)
            for yy in range(NY):
                t = dot(parts, gf[2 * yy + k])
                tbp[2 * yy + k] = t[0:RANK] + t[RANK : 2 * RANK] + t[2 * RANK :]
        tbi[q] = tbp[q]
        r_tb.start(lambda i: tbp.at[i])

    def send_tokens():
        r_ns.wait()
        low = []
        for k in range(2):
            acc = None
            for yy in range(NY):
                i = 2 * yy + k
                s = (gf[i].astype(F32) * ns[i, 1:2]).astype(BF16)
                scaled[i] = s
                t = dot(s, bf[yy, k], NT)
                acc = t if acc is None else acc + t
            low.append(acc)
        lowf = jnp.concatenate(low, axis=1)
        lowo[...] = lowf.astype(BF16)
        lowt = lowf.T.astype(BF16)
        for xx in range(NX):
            tpp[xx] = dot(lowt, actsf[:, xx * ROWS : (xx + 1) * ROWS])
        tpi[x] = tpp[x]
        r_tpx.start(lambda i: tpp.at[i])

    def sum_tokens_x():
        r_tpx.wait()
        tps[...] = total(tpi, NX).reshape(NZ, 8, ROWS)
        tpzi[z] = tps[z]
        r_tpz.start(lambda i: tps.at[i])

    def sum_tokens_z():
        r_tpz.wait()
        tpg[z] = total(tpzi, NZ)
        r_tpg.start(lambda _: tpg.at[z])

    def sum_products_q():
        r_tb.wait()
        token_b = total(tbi, NQ)
        for g in range(NZ):
            ctp[g, 0:4] = across[4 * g : 4 * g + 4]
            ctp[g, 4:8] = token_b[4 * g : 4 * g + 4]
        cti[z] = ctp[z]
        r_ctz.start(lambda i: ctp.at[i])

    def sum_products_z():
        r_ctz.wait()
        ctx[x] = total(cti, NZ)
        r_ctx.start(lambda _: ctx.at[x])

    def sum_products_x():
        r_ctx.wait()
        ctz[z] = total(ctx, NX)
        r_ctg.start(lambda _: ctz.at[z])

    def column_sums(way, s):
        bx_wait(way, s)
        forward(origin(way, s))

    ring_b(1)
    bx_forward(0, 0)
    ring_a(1, lambda: None, cot_relay)
    ring_b(2)
    bx_forward(0, 1)
    bx_forward(1, 1)
    r_b.wait()
    cot_wait()
    send_token_b()
    send_tokens()
    ring_a(2, lambda: column_sums(0, 0), lambda: None, sum_products_q)
    ring_b(3)
    bx_forward(0, 2)
    bx_forward(1, 2)
    sum_tokens_x()
    column_sums(0, 1)
    column_sums(1, 1)
    ring_a(3)
    ring_b(4)
    bx_forward(0, 3)
    bx_forward(1, 3)
    column_sums(0, 2)
    column_sums(1, 2)
    ring_a(4)
    column_sums(0, 3)
    column_sums(1, 3)
    bx4_wait()
    forward(origin(0, 4))

    r_mox = Ring(NX, x, xpeer, mox)
    r_moz = Ring(NZ, z, zpeer, moz)
    r_moq = Ring(NQ, q, qpeer, moq)
    extra = []
    for i in range(NQ):
        extra.append(jnp.sum(tbp[i] * bf[i // 2, i % 2].astype(F32), axis=0, keepdims=True))
    mox[x] = momt[...] + jnp.concatenate(extra, axis=0)
    r_mox.start(lambda _: mox.at[x])

    def backward(xx):
        acc = dot(lowo[...], ah[:, xx * ROWS : (xx + 1) * ROWS])
        for zi in range(NZ):
            acc = acc + dot(scaled[zi], w[zi, xx], NT)
        gxb[:, xx * ROWS : (xx + 1) * ROWS] = acc.astype(BF16)

    sum_tokens_z()
    sum_products_z()
    backward(0)
    r_mox.wait()
    moz[z] = total(mox, NX)
    r_moz.start(lambda _: moz.at[z])
    sum_products_x()
    backward(1)
    backward(2)
    r_moz.wait()
    moq[q] = total(moz, NZ)
    r_moq.start(lambda _: moq.at[q])
    r_ctg.wait()
    ctc[p] = ctz[...]
    s_ctc, r_ctc = sems("send"), sems("recv")
    copy(ctc.at[p], ctc.at[p], s_ctc, r_ctc, core).start()
    sent(ctc.at[p], s_ctc)
    backward(3)

    s_gx, r_gx = sems("send"), sems("recv")
    copy(gxb.at[others, :], gx_out.at[:, my_half], s_gx, r_gx, core).start()
    sent(gxb.at[others, :], s_gx)
    stores = [pltpu.make_async_copy(gxb.at[mine, :], gx_out.at[:, my_half], lsem.at[sems("local")])]
    stores[0].start()

    r_moq.wait()
    moment = total(moq, NQ)
    norm_all = jnp.concatenate([ns[i, 0:1] for i in range(NQ)], axis=0)
    scal_all = jnp.concatenate([ns[i, 1:2] for i in range(NQ)], axis=0)
    grad_mag = moment / norm_all
    factor = scal_all * grad_mag / norm_all
    momt[...] = grad_mag

    for k in range(2):
        inner = None
        for yy in range(NY):
            i = 2 * yy + k
            two = jnp.concatenate(pieces(bf[yy, k].astype(F32) * factor[i : i + 1], 2), axis=0)
            wts[i] = two
            t = dot(two, bf[yy, k], NT)
            inner = t if inner is None else inner + t
        inr[k] = jnp.concatenate(pieces(inner[0:RANK] + inner[RANK:], 2), axis=0)

    s_gay, s_gax, s_gac = sems("send"), sems("send"), sems("send")
    r_gay, r_gax, r_gac = sems("recv", NY), sems("recv", 3 * NY), sems("recv", NX)
    l_ga = sems("local")

    def ga_block(d, of_core, j):
        return gaf.at[2 * lax.rem(y - d + NY, NY) + of_core, lax.rem(x - j + NX, NX)]

    def ga_store(d, of_core, j):
        block = ga_block(d, of_core, j)
        first = (2 * lax.rem(y - d + NY, NY) + of_core) * HALF + lax.rem(x - j + NX, NX) * ROWS
        for k in range(2):
            dst = ga_out.at[k, :, pl.ds(pl.multiple_of(first, 128), ROWS)]
            pltpu.make_async_copy(block.at[pl.ds(k * RANK, RANK), :], dst, lsem.at[l_ga]).start()

    def ga_core(d, j):
        here = ga_block(d, p, j)
        copy(here, here, s_gac, r_gac + j, core).start()
        ga_store(d, p, j)

    def ga_x(d):
        here = ga_block(d, p, 0)
        for turn in range(2):
            copy(here, here, s_gax, r_gax + 3 * d + turn, xpeer(1 if turn == 0 else NX - 1)).start()
        ga_core(d, 0)

    r_tpg.wait()
    tokens = tpg[...].reshape(2 * RANK, ROWS)
    span = pl.ds(pl.multiple_of(x * ROWS, ROWS), ROWS)
    for k in range(2):
        acc = dot(inr[k], ah[k * RANK : (k + 1) * RANK, span])
        for yy in range(NY):
            acc = acc + dot(wts[2 * yy + k], w[2 * yy + k, x], NT)
        rows = slice(k * RANK, (k + 1) * RANK)
        gaf[q, x, rows, :] = (tokens[rows] - (acc[0:RANK] + acc[RANK:])).astype(BF16)
    here_ga = gaf.at[q, x]
    each(1, NY, lambda d: copy(here_ga, here_ga, s_gay, r_gay + d, ypeer(d)).start())
    ga_x(0)

    arrived(ctc.at[1 - p], r_ctc)
    for k in range(2):
        i = 2 * y + k
        norm_k = ns[i, 0:1]
        scal_k = ns[i, 1:2]
        gm_k = momt[pl.ds(i, 1), :]
        gm_out[k : k + 1] = gm_k
        ratio = gm_k / norm_k
        for g in range(NZ):
            gb_out[k, 4 * g : 4 * g + 4] = scal_k * (ctc[k, g, 4:8] - ctc[k, g, 0:4] * ratio)

    for d in (1, 3, 2):
        arrived(ga_block(d, p, 0), r_gay + d)
        ga_x(d)
    for d in (0, 1, 3, 2):
        for turn in range(2):
            j = 1 if turn == 0 else NX - 1
            here = ga_block(d, p, j)
            arrived(here, r_gax + 3 * d + turn)
            if (d in (0, 2)) == (turn == 0):
                copy(here, here, s_gax, r_gax + 3 * d + 2, xpeer(1 if turn == 0 else NX - 1)).start()
            ga_core(d, j)
    for d in (0, 1, 3, 2):
        arrived(ga_block(d, p, 2), r_gax + 3 * d + 2)
        ga_core(d, 2)
    for j in (0, 1, 3, 2):
        arrived(gaf.at[0], r_gac + j)
        for d in range(NY):
            ga_store(d, 1 - p, j)
    arrived(gxb.at[others, :], r_gx)
    for store in stores:
        store.wait()
    sent(gaf.at[0, pl.ds(0, 3)], s_gay)
    sent(gaf.at[pl.ds(0, 3)], s_gax)
    sent(gaf.at[pl.ds(0, NY)], s_gac)
    pltpu.make_async_copy(gaf, gaf, lsem.at[l_ga]).wait()
    assert counts == limits, counts
    for final in finals:
        final()


SENDS, RECVS, LOCALS = 27, 110, 9


def finish(gx, ga, gb, gm):
    cuts = 4

    def widen(gx_in, ga_in, gb_in, gm_in, gx_to, ga_to, gb_to, gm_to):
        gx_to[...] = gx_in[...]
        ga_to[...] = ga_in[...].astype(F32)
        gb_to[...] = gb_in[...]
        gm_to[...] = gm_in[...]

    specs = [
        pl.BlockSpec((TOK, FEAT // cuts), lambda i: (0, i)),
        pl.BlockSpec((2, RANK, NQ * HALF // cuts), lambda i: (0, 0, i)),
        pl.BlockSpec((2, RANK, COLS), lambda i: (0, 0, 0)),
        pl.BlockSpec((2, COLS), lambda i: (0, 0)),
    ]
    return pl.pallas_call(
        widen,
        grid=(cuts,),
        out_shape=tuple(
            jax.ShapeDtypeStruct(v.shape, F32 if v is ga else v.dtype) for v in (gx, ga, gb, gm)
        ),
        in_specs=specs,
        out_specs=tuple(specs),
        compiler_params=pltpu.CompilerParams(vmem_limit_bytes=62 * 2**20),
    )(gx, ga, gb, gm)


def on_device(acts, cot, base, adapter_a, adapter_b, magnitude):
    at = jnp.swapaxes(adapter_a, 1, 2)
    vm = pl.BlockSpec(memory_space=pltpu.VMEM)
    hbm = pl.BlockSpec(memory_space=pl.ANY)
    scratch = [
        ((NZ, NX, ROWS, COLS), BF16),
        ((TOK2, HALF), BF16),
        ((NQ, TOK2, COLS), BF16),
        ((NQ, TOK2, COLS), BF16),
        ((NY, 2, RANK, COLS), BF16),
        ((2 * RANK, HALF), BF16),
        ((RANK, ROWS), BF16),
        ((ROWS, COLS), BF16),
        ((NX, 8, COLS), F32),
        ((NZ, 8, COLS), F32),
        ((NQ, 8, COLS), F32),
        ((NQ, RANK, COLS), F32),
        ((NQ, RANK, COLS), F32),
        ((NZ, 8, COLS), F32),
        ((NZ, 8, COLS), F32),
        ((NX, 8, COLS), F32),
        ((NZ, 8, COLS), F32),
        ((2, NZ, 8, COLS), F32),
        ((NX, 2 * RANK, ROWS), F32),
        ((NX, 2 * RANK, ROWS), F32),
        ((NZ, 8, ROWS), F32),
        ((NZ, 8, ROWS), F32),
        ((NZ, 8, ROWS), F32),
        ((NX, 8, COLS), F32),
        ((NZ, 8, COLS), F32),
        ((NQ, 8, COLS), F32),
        ((NQ, NX, 2 * RANK, ROWS), BF16),
        ((TOK2, HALF), BF16),
        ((TOK2, 2 * RANK), BF16),
        ((NQ, COLS), F32),
        ((NQ, 2 * RANK, COLS), BF16),
        ((2, 2 * RANK, RANK), BF16),
    ]
    gx, ga, gb, gm = pl.pallas_call(
        kernel,
        out_shape=(
            jax.ShapeDtypeStruct((TOK, FEAT), BF16),
            jax.ShapeDtypeStruct((2, RANK, NQ * HALF), BF16),
            jax.ShapeDtypeStruct((2, RANK, COLS), F32),
            jax.ShapeDtypeStruct((2, COLS), F32),
        ),
        in_specs=[hbm, hbm, hbm, hbm, vm, vm],
        out_specs=(hbm, hbm, vm, vm),
        scratch_shapes=[pltpu.VMEM(shape, dtype) for shape, dtype in scratch]
        + [pltpu.SemaphoreType.DMA((n,)) for n in (SENDS, RECVS, LOCALS)],
        compiler_params=pltpu.CompilerParams(
            collective_id=0, has_side_effects=True, vmem_limit_bytes=56 * 2**20
        ),
        cost_estimate=pl.CostEstimate(flops=5 * 10**9, bytes_accessed=8 * 10**6, transcendentals=0),
    )(acts, cot, base, at, adapter_b, magnitude)
    gx, ga, gb, gm = finish(gx, ga, gb, gm)
    return gx, jnp.swapaxes(ga, 1, 2), gb, gm


def solution(mesh):
    in_specs = (
        P(("dp", "fsdp"), "col"),
        P(None, ("dp", "fsdp"), "col"),
        P(None, "fsdp", "col"),
        P(),
        P(None, None, "col"),
        P(None, "col"),
    )
    out_specs = (P(("dp", "fsdp"), "col"), P(), P(None, None, "col"), P(None, "col"))
    return jax.shard_map(
        on_device, mesh=mesh, in_specs=in_specs, out_specs=out_specs, check_vma=False
    )
```

time: 124 us -> 101 us (0.81)
  Pallas kernels: 118 us -> 99.8 us
  other arithmetic: 3.37 us -> 0 us
  local copies, waits for them, and re-layouts: 2.23 us -> 0 us
    pallas_call x1, Pallas kernels: 118 us -> 95.4 us  [on_device(): pl.pallas_call(kernel, out_shape=(jax.ShapeDtypeStruct((TOK, FEAT), BF16)...]
    pallas_call x0 -> x1, Pallas kernels: none -> 4.35 us  [finish(): pl.pallas_call(widen, grid=(cuts,), out_shape=tuple((jax.ShapeDtypeStruct...]
    transpose x1 -> x0, other arithmetic: 3.37 us -> none  [on_device(): return (gx, jnp.swapaxes(ga.astype(F32), 1, 2), gb, gm)]
    unnamed x9 -> x0, local copies, waits for them, and re-layouts: 2.23 us -> none
where the time goes in v2:
time: 101 us; the launch traced here: 100 us
  Pallas kernels  99.8 us (99%)
    pallas_call x1, Pallas kernels, on_device(): pl.pallas_call(kernel, out_shape=(jax.ShapeDtypeStruct((TOK, FEAT), BF16)...  95.4 us
    pallas_call x1, Pallas kernels, finish(): pl.pallas_call(widen, grid=(cuts,), out_shape=tuple((jax.ShapeDtypeStruct...  4.35 us

profile of v2, /device:TPU:1, one launch (start us, length us, event | category | flops | bytes accessed | tf_op | source)
XLA Modules:
  0.0 100.4 jit_solution(5681158916875848355)
XLA Ops:
  0.6 95.4 %shard_map.93 = (bf16[192,3072]{1,0:T(8,128)(2,1)}, bf16[2,32,12288]{2,1,0:T(8,128)(2,1)}, f32[2,32,256]{2,1,0:T(8,128)}, f32[2,256]{1,0:T(2,128)}) custom-call(bf16[192,3072]{1,0:T(8,128)(2,1)} %acts.1, bf16[2,192,256]{2,1,0:T(8,128)(2,1)} %cot.1, bf16[2,384,256]{2,1,0:T(8,128)(2,1)} %base.1, bf16[2,32,12288]{2,1,0:T(8,128)(2,1)} %bitcast.3, ...), custom_call_target="tpu_custom_call" | custom-call | flops 5000000000 | bytes 8000000 | tf_op jit(solution)/shard_map/pallas_call | solution.py:658
  96.1 4.3 %shard_map.94 = (bf16[192,3072]{1,0:T(8,128)(2,1)}, f32[2,32,12288]{2,1,0:T(8,128)}, f32[2,32,256]{2,1,0:T(8,128)}, f32[2,256]{1,0:T(2,128)}) custom-call(bf16[192,3072]{1,0:T(8,128)(2,1)} %get-tuple-element.12.gx_in, bf16[2,32,12288]{2,1,0:T(8,128)(2,1)} %get-tuple-element.13.ga_in, f32[2,32,256]{2,1,0:T(8,128)} %get-tuple-element.14.gb_in, ...), custom_call_target="tpu_custom_call" | custom-call | tf_op jit(solution)/shard_map/pallas_call | solution.py:608

commit v3 on v2

v3 whole, which is shorter than its diff:
```python
import functools

import jax
import jax.numpy as jnp
from jax import lax
from jax.experimental import pallas as pl
from jax.experimental.pallas import tpu as pltpu
from jax.sharding import PartitionSpec as P

MESH = pl.DeviceIdType.MESH
F32 = jnp.float32
BF16 = jnp.bfloat16

NX, NZ, NY = 4, 8, 4
NQ = 2 * NY

TOK = 192
PAIR = 4 * TOK
FEAT = 3072
HALF = FEAT // 2
COLS = 256
ROWS = 384
WORK = 2 * ROWS
RANK = 32
CUT = 160

NT = (((1,), (1,)), ((), ()))
TN = (((0,), (0,)), ((), ()))
NN = (((1,), (0,)), ((), ()))


def dot(a, b, dims=NN):
    return lax.dot_general(a, b, dims, preferred_element_type=F32)


def pieces(value, count):
    out = []
    for _ in range(count):
        part = value.astype(BF16)
        out.append(part)
        value = value - part.astype(F32)
    return out


def total(ref, count):
    value = ref[0]
    for i in range(1, count):
        value = value + ref[i]
    return value


def kernel(
    acts, cot, base, at, b, mag,
    gx_out, ga_out, gb_out, gm_out,
    w, actsf, gf, scaled, bf, ah, ar, mybase,
    sqx, sqz, ns, tbp, tbi, ctp, cti, ctx, ctz, ctc,
    tpp, tpi, tps, tpzi, tpg, mox, moz, moq, gaf, gxb, lowo, momt, wts, inr,
    ssem, rsem, lsem,
):
    p = lax.axis_index("dp")
    f = lax.axis_index("fsdp")
    y = lax.axis_index("col")
    x = lax.rem(f, NX)
    z = lax.div(f, NX)
    q = 2 * y + p

    def at_xz(nx, nz):
        return (p, nz * NX + nx, y)

    def at_q(nq):
        return (lax.rem(nq, 2), f, lax.div(nq, 2))

    xpeer = lambda d: at_xz(lax.rem(x + d, NX), z)
    zpeer = lambda d: at_xz(x, lax.rem(z + d, NZ))
    qpeer = lambda d: at_q(lax.rem(q + d, NQ))
    ypeer = lambda d: (p, f, lax.rem(y + d, NY))
    core = (1 - p, f, y)
    h = lax.rem(lax.div(x + 1, 2), 2)
    partner = (p, f + 1 - 2 * lax.rem(x, 2), y)
    cross = (1 - p, f + 1 - 2 * lax.rem(x, 2), y)
    across_x = at_xz(NX - 1 - x, z)
    own_slot = lax.div(x, 2)
    slot_of = lambda jj: lax.rem(own_slot + jj, 2)

    def shift(c):
        k, half = lax.rem(c, 2), lax.div(c, 2)
        return lax.rem((1 - k) * half + k * (4 + (4 - half) * jnp.minimum(half, 1)), NZ)

    def chunk_at(position):
        step = lax.rem(position - q + NZ, NZ)
        far = lax.div(step, 4)
        return (1 - far) * 2 * step + far * lax.rem(17 - 2 * step, NZ)

    target = (lax.rem(z, 2), lax.rem(z + shift(q), NZ) * NX + x, lax.div(z, 2))
    own = chunk_at(z)
    source = (lax.rem(own, 2), q * NX + x, lax.div(own, 2))
    fixed = jnp.logical_and(own == q, z == q)

    counts = {"send": 0, "recv": 0, "local": 0}
    limits = {"send": SENDS, "recv": RECVS, "local": LOCALS}
    finals = []

    def sems(kind, n=1):
        counts[kind] += n
        assert counts[kind] <= limits[kind]
        return counts[kind] - n

    def copy(src, dst, send, recv, dev):
        return pltpu.make_async_remote_copy(
            src_ref=src, dst_ref=dst, send_sem=ssem.at[send], recv_sem=rsem.at[recv],
            device_id=dev, device_id_type=MESH,
        )

    def arrived(ref, recv):
        copy(ref, ref, 0, recv, core).wait_recv()

    def sent(ref, send):
        finals.append(lambda: copy(ref, ref, send, 0, core).wait_send())

    def each(lo, hi, body):
        def step(i, carry):
            body(i)
            return carry

        lax.fori_loop(lo, hi, step, 0)

    class Ring:
        def __init__(self, n, me, peer, dst):
            self.n, self.me, self.peer, self.dst = n, me, peer, dst
            self.send, self.recv = sems("send"), sems("recv")

        def start(self, src):
            def one(d):
                block = src(lax.rem(self.me + d, self.n))
                copy(block, self.dst.at[self.me], self.send, self.recv, self.peer(d)).start()

            each(1, self.n, one)
            sent(self.dst.at[pl.ds(0, self.n - 1)], self.send)

        def wait(self):
            arrived(self.dst.at[pl.ds(0, self.n - 1)], self.recv)

    def tokens_of(core_of, half_of):
        return pl.ds(pl.multiple_of(core_of * 2 * TOK + half_of * TOK, TOK), TOK)

    mine = tokens_of(p, h)
    my_core = pl.ds(pl.multiple_of(p * 2 * TOK, TOK), 2 * TOK)

    def shard(core_of, half_of, j):
        return pl.ds(pl.multiple_of(core_of * HALF + (half_of + j * (3 - 2 * half_of)) * ROWS, 128), ROWS)

    bar = pltpu.get_barrier_semaphore()
    each(1, NX, lambda d: pl.semaphore_signal(bar, inc=1, device_id=xpeer(d), device_id_type=MESH))
    each(1, NZ, lambda d: pl.semaphore_signal(bar, inc=1, device_id=zpeer(d), device_id_type=MESH))
    each(1, NQ, lambda d: pl.semaphore_signal(bar, inc=1, device_id=qpeer(d), device_id_type=MESH))

    pl.semaphore_signal(bar, inc=1, device_id=cross, device_id_type=MESH)

    @pl.when(jnp.logical_not(fixed))
    def _():
        pl.semaphore_signal(bar, inc=1, device_id=source, device_id_type=MESH)

    loads = [
        pltpu.make_async_copy(base.at[p], mybase, lsem.at[sems("local")]),
        pltpu.make_async_copy(at.at[p, :, pl.ds(pl.multiple_of(f * ROWS, ROWS), ROWS)], ar, lsem.at[sems("local")]),
    ]
    for k in range(2):
        for j in range(2):
            cols = pl.ds(pl.multiple_of(q * HALF + (h + j * (3 - 2 * h)) * ROWS, 128), ROWS)
            dst = ah.at[pl.ds(k * RANK, RANK), pl.ds(j * ROWS, ROWS)]
            loads.append(pltpu.make_async_copy(at.at[k, :, cols], dst, lsem.at[sems("local")]))
        loads.append(pltpu.make_async_copy(cot.at[k], gf.at[2 * y + k, mine, :], lsem.at[sems("local")]))
    for j in range(2):
        dst = actsf.at[mine, pl.ds(j * ROWS, ROWS)]
        loads.append(pltpu.make_async_copy(acts.at[:, shard(p, h, j)], dst, lsem.at[sems("local")]))
    for load in loads:
        load.start()

    @pl.when(jnp.logical_not(fixed))
    def _():
        pl.semaphore_wait(bar, NX + NZ + NQ - 1)

    @pl.when(fixed)
    def _():
        pl.semaphore_wait(bar, NX + NZ + NQ - 2)

    PARTS = ((0, CUT), (CUT, ROWS))
    s_swap, r_swap = sems("send"), sems("recv", 2)

    def swap_copy(i):
        lo, hi = PARTS[i]
        return copy(base.at[p, pl.ds(lo, hi - lo), :], w.at[q, own_slot, pl.ds(lo, hi - lo), :], s_swap, r_swap + i, target)

    @pl.when(jnp.logical_not(fixed))
    def _():
        swap_copy(1).start()
        swap_copy(0).start()

    def wait_swap(i):
        lo, hi = PARTS[i]

        @pl.when(jnp.logical_not(fixed))
        def _():
            arrived(w.at[own, own_slot, pl.ds(lo, hi - lo), :], r_swap + i)

        @pl.when(fixed)
        def _():
            w[own, own_slot, lo:hi, :] = mybase[lo:hi, :]

    def final_swap():
        @pl.when(jnp.logical_not(fixed))
        def _():
            copy(mybase, mybase, s_swap, 0, target).wait_send()

    finals.append(final_swap)
    r_sqx = Ring(NX, x, xpeer, sqx)
    r_sqz = Ring(NZ, z, zpeer, sqz)
    r_ns = Ring(NQ, q, qpeer, ns)
    for load in loads:
        load.wait()
    composed = mybase[...].astype(F32) + dot(ar[...], b[p], TN)
    sqx[x] = jnp.broadcast_to(jnp.sum(composed * composed, axis=0, keepdims=True), (8, COLS))
    across = functools.reduce(lambda u, v: u + v, [dot(ar[...], c) for c in pieces(composed, 3)])

    r_sqx.start(lambda _: sqx.at[x])

    s_gotx, s_goty, s_gotc = sems("send"), sems("send"), sems("send")
    r_gotx, r_goty, r_gotc = sems("recv"), sems("recv", 6), sems("recv")
    parts_of_pair = (mine, tokens_of(p, 1 - h))
    two = gf.at[0, my_core, :]
    def cot_y(i, source=None):
        for turn in range(2):
            for k in range(2):
                there = gf.at[2 * y + k, parts_of_pair[i], :]
                src = there if source is None else source.at[k]
                copy(src, there, s_goty, r_goty + 3 * i + turn, ypeer(1 if turn == 0 else NY - 1)).start()

    def cot_forward(i):
        for turn in range(2):
            arrived(two, r_goty + 3 * i + turn)
            yy = lax.rem(y + (NY - 1 if turn == 0 else 1), NY)
            here = gf.at[2 * yy + turn, parts_of_pair[i], :]
            copy(here, here, s_goty, r_goty + 3 * i + 2, ypeer(1 if turn == 0 else NY - 1)).start()

    def cot_core(d):
        for k in range(2):
            here = gf.at[2 * lax.rem(y - d + NY, NY) + k, my_core, :]
            copy(here, here, s_gotc, r_gotc, core).start()

    cot_y(0, cot)
    for k in range(2):
        copy(cot.at[k], gf.at[2 * y + k, mine, :], s_gotx, r_gotx, partner).start()
    sent(two, s_gotx)

    sent(gf.at[pl.ds(0, NY - 1)], s_goty)
    sent(gf.at[pl.ds(0, NY)], s_gotc)

    def cot_start():
        arrived(two, r_gotx)
        cot_y(1)
        cot_core(0)

    def cot_relay():
        cot_forward(1)
        cot_core(1)
        cot_core(3)

    def cot_relay_last():
        for i in range(2):
            arrived(two, r_goty + 3 * i + 2)
        cot_core(2)

    def cot_wait():
        arrived(gf.at[pl.ds(0, NY)], r_gotc)

    s_acts, r_acts = sems("send"), sems("recv")

    def acts_start(j):
        for core_of, half_of, dev in ((p, 1 - h, partner), (1 - p, 1 - h, cross), (1 - p, h, core)):
            dst = actsf.at[mine, pl.ds(j * ROWS, ROWS)]
            copy(acts.at[:, shard(core_of, half_of, j)], dst, s_acts, r_acts, dev).start()

    acts_start(0)
    sent(actsf.at[pl.ds(0, 3 * TOK), :], s_acts)

    def acts_wait():
        arrived(actsf.at[pl.ds(0, 3 * TOK), :], r_acts)

    r_b = Ring(NY, y, ypeer, bf)
    bf[y] = b[...]
    r_b.start(lambda i: bf.at[y])

    s_ax, s_az, s_bz, s_bx = sems("send"), sems("send"), sems("send"), sems("send")
    r_ax, r_az, r_bz = sems("recv"), sems("recv", 2 * 8), sems("recv", 8)
    r_bx, r_bx4 = sems("recv", 7), sems("recv")
    b_lo, b_n = CUT, ROWS - CUT
    b_half = b_n // 2

    def ring_rows(part, way, s):
        lo, hi = PARTS[part]
        if s < 3:
            return lo, hi - lo
        half = (hi - lo) // 2
        return lo + way * half, half

    def origin(way, s):
        return chunk_at(lax.rem(z - s + NZ, NZ) if way == 0 else lax.rem(z + s, NZ))

    def z_sem(part, j, way, s):
        return (r_az + (j * 2 + way) * 4 + s) if part == 0 else (r_bz + way * 4 + s)

    def z_start(part, j, way, s):
        lo, n = ring_rows(part, way, s)
        here = w.at[origin(way, s), slot_of(j), pl.ds(lo, n), :]
        send = s_az if part == 0 else s_bz
        copy(here, here, send, z_sem(part, j, way, s), zpeer(1 if way == 0 else NZ - 1)).start()

    def z_arrival(part, j, way, s):
        lo, n = ring_rows(part, way, s)
        arrived(w.at[origin(way, s + 1), slot_of(j), pl.ds(lo, n), :], z_sem(part, j, way, s))

    sent(w.at[pl.ds(0, 7), :, pl.ds(0, CUT), :], s_az)
    sent(w.at[pl.ds(0, 7), 0, pl.ds(b_lo, b_n), :], s_bz)
    sent(w.at[pl.ds(0, 4), :, pl.ds(b_lo, b_n), :], s_bx)
    sent(w.at[0, 0, pl.ds(0, CUT), :], s_ax)

    def bx_sem(way, s):
        return r_bx + (0 if s == 0 else 1 + way * 3 + s - 1)

    def bx_start(way, s):
        here = w.at[origin(way, s), own_slot, pl.ds(b_lo, b_n), :]
        copy(here, here, s_bx, bx_sem(way, s), across_x).start()

    def bx_wait(way, s):
        arrived(w.at[origin(way, s), slot_of(1), pl.ds(b_lo, b_n), :], bx_sem(way, s))

    def bx4_start(way):
        here = w.at[origin(way, 4), own_slot, pl.ds(b_lo + way * b_half, b_half), :]
        copy(here, here, s_bx, r_bx4, across_x).start()

    def bx4_wait():
        arrived(w.at[origin(0, 4), slot_of(1), pl.ds(b_lo, b_n), :], r_bx4)

    r_sqx.wait()
    sqz[z] = total(sqx, NX)
    r_sqz.start(lambda _: sqz.at[z])
    cot_start()
    wait_swap(1)
    for way in range(2):
        z_start(1, 0, way, 0)
    wait_swap(0)
    here_a = w.at[own, own_slot, pl.ds(0, CUT), :]
    copy(here_a, here_a, s_ax, r_ax, across_x).start()
    for way in range(2):
        z_start(0, 0, way, 0)
    bx_start(0, 0)
    acts_start(1)
    cot_forward(0)
    r_sqz.wait()
    norms = jnp.sqrt(total(sqz, NZ)[0:1])
    ns[q, 0:1] = norms
    ns[q, 1:2] = mag[pl.ds(p, 1), :] / norms
    r_ns.start(lambda _: ns.at[q])
    def ring_b(s):
        for way in range(2):
            z_arrival(1, 0, way, s - 1)
            if s < 4:
                z_start(1, 0, way, s)
                bx_start(way, s)
            else:
                bx4_start(way)

    def ring_a(j, s):
        for way in range(2):
            z_arrival(0, j, way, s - 1)
            if s < 4:
                z_start(0, j, way, s)

    def forward(zi):
        out = dot(actsf[...], w[zi].reshape(WORK, COLS))
        momt[pl.ds(zi, 1), :] = jnp.sum(out * gf[zi].astype(F32), axis=0, keepdims=True)

    r_tb = Ring(NQ, q, qpeer, tbi)
    r_ctz = Ring(NZ, z, zpeer, cti)
    r_ctx = Ring(NX, x, xpeer, ctx)
    r_ctg = Ring(NZ, z, zpeer, ctz)
    s_tpx, r_tpx = sems("send"), sems("recv")
    r_tpz = Ring(NZ, z, zpeer, tpzi)
    r_tpg = Ring(NZ, z, zpeer, tpg)

    def send_token_b():
        low_in = dot(ah[...], actsf[...], NT)
        for k in range(2):
            parts = jnp.concatenate(pieces(low_in[k * RANK : (k + 1) * RANK], 3), axis=0)
            for yy in range(NY):
                t = dot(parts, gf[2 * yy + k])
                tbp[2 * yy + k] = t[0:RANK] + t[RANK : 2 * RANK] + t[2 * RANK :]
        tbi[q] = tbp[q]
        r_tb.start(lambda i: tbp.at[i])

    def send_tokens():
        r_ns.wait()
        low = []
        for k in range(2):
            acc = None
            for yy in range(NY):
                i = 2 * yy + k
                s = (gf[i].astype(F32) * ns[i, 1:2]).astype(BF16)
                scaled[i] = s
                t = dot(s, bf[yy, k], NT)
                acc = t if acc is None else acc + t
            low.append(acc)
        lowf = jnp.concatenate(low, axis=1)
        lowo[...] = lowf.astype(BF16)
        lowt = lowf.T.astype(BF16)
        for j in range(2):
            tpp[j] = dot(lowt, actsf[:, j * ROWS : (j + 1) * ROWS])
        copy(tpp.at[slot_of(1)], tpi, s_tpx, r_tpx, across_x).start()
        sent(tpi, s_tpx)

    def sum_tokens_x():
        arrived(tpi, r_tpx)
        tps[...] = (tpp[own_slot] + tpi[...]).reshape(NZ, 8, ROWS)
        tpzi[z] = tps[z]
        r_tpz.start(lambda i: tps.at[i])

    def sum_tokens_z():
        r_tpz.wait()
        tpg[z] = total(tpzi, NZ)
        r_tpg.start(lambda _: tpg.at[z])

    def sum_products_q():
        r_tb.wait()
        token_b = total(tbi, NQ)
        for g in range(NZ):
            ctp[g, 0:4] = across[4 * g : 4 * g + 4]
            ctp[g, 4:8] = token_b[4 * g : 4 * g + 4]
        cti[z] = ctp[z]
        r_ctz.start(lambda i: ctp.at[i])

    def sum_products_z():
        r_ctz.wait()
        ctx[x] = total(cti, NZ)
        r_ctx.start(lambda _: ctx.at[x])

    def sum_products_x():
        r_ctx.wait()
        ctz[z] = total(ctx, NX)
        r_ctg.start(lambda _: ctz.at[z])

    def column_sums(way, s):
        bx_wait(way, s)
        forward(origin(way, s))

    ring_b(1)
    ring_a(0, 1)
    arrived(w.at[own, slot_of(1), pl.ds(0, CUT), :], r_ax)
    for way in range(2):
        z_start(0, 1, way, 0)
    cot_relay()
    ring_b(2)
    ring_a(0, 2)
    ring_a(1, 1)
    r_b.wait()
    cot_relay_last()
    cot_wait()
    acts_wait()
    send_tokens()
    ring_b(3)
    ring_a(0, 3)
    column_sums(0, 0)
    send_token_b()
    ring_a(1, 2)
    column_sums(0, 1)
    column_sums(1, 1)
    ring_b(4)
    ring_a(0, 4)
    column_sums(0, 2)
    column_sums(1, 2)
    ring_a(1, 3)
    column_sums(0, 3)
    column_sums(1, 3)
    sum_tokens_x()
    sum_products_q()
    ring_a(1, 4)
    bx4_wait()
    forward(origin(0, 4))

    r_mox = Ring(NX, x, xpeer, mox)
    r_moz = Ring(NZ, z, zpeer, moz)
    r_moq = Ring(NQ, q, qpeer, moq)
    extra = []
    for i in range(NQ):
        extra.append(jnp.sum(tbp[i] * bf[i // 2, i % 2].astype(F32), axis=0, keepdims=True))
    mox[x] = momt[...] + jnp.concatenate(extra, axis=0)
    r_mox.start(lambda _: mox.at[x])

    s_gx, r_gx = sems("send"), sems("recv")
    l_gx = sems("local")

    def backward(j):
        cols = slice(j * ROWS, (j + 1) * ROWS)
        acc = dot(lowo[...], ah[:, cols])
        for zi in range(NZ):
            acc = acc + dot(scaled[zi], w[zi, j], NT)
        gxb[:, cols] = acc.astype(BF16)
        there = gx_out.at[:, shard(p, h, j)]
        part = pl.ds(j * ROWS, ROWS)
        for core_of, half_of, dev in ((p, 1 - h, partner), (1 - p, 1 - h, cross), (1 - p, h, core)):
            copy(gxb.at[tokens_of(core_of, half_of), part], there, s_gx, r_gx, dev).start()
        pltpu.make_async_copy(gxb.at[mine, part], there, lsem.at[l_gx]).start()

    backward(0)
    r_mox.wait()
    moz[z] = total(mox, NX)
    r_moz.start(lambda _: moz.at[z])
    backward(1)
    sum_tokens_z()
    r_moz.wait()
    moq[q] = total(moz, NZ)
    r_moq.start(lambda _: moq.at[q])
    sum_products_z()
    r_moq.wait()
    moment = total(moq, NQ)
    norm_all = jnp.concatenate([ns[i, 0:1] for i in range(NQ)], axis=0)
    scal_all = jnp.concatenate([ns[i, 1:2] for i in range(NQ)], axis=0)
    grad_mag = moment / norm_all
    factor = scal_all * grad_mag / norm_all
    momt[...] = grad_mag

    for k in range(2):
        inner = None
        for yy in range(NY):
            i = 2 * yy + k
            two = jnp.concatenate(pieces(bf[yy, k].astype(F32) * factor[i : i + 1], 2), axis=0)
            wts[i] = two
            t = dot(two, bf[yy, k], NT)
            inner = t if inner is None else inner + t
        inr[k] = jnp.concatenate(pieces(inner[0:RANK] + inner[RANK:], 2), axis=0)

    s_gay, s_gax, s_gac = sems("send"), sems("send"), sems("send")
    r_gay, r_gax, r_gac = sems("recv", NY), sems("recv", 3 * NY), sems("recv", NX)
    l_ga = sems("local")

    def ga_block(d, of_core, j):
        return gaf.at[2 * lax.rem(y - d + NY, NY) + of_core, lax.rem(x - j + NX, NX)]

    def ga_store(d, of_core, j):
        block = ga_block(d, of_core, j)
        first = (2 * lax.rem(y - d + NY, NY) + of_core) * HALF + lax.rem(x - j + NX, NX) * ROWS
        for k in range(2):
            dst = ga_out.at[k, :, pl.ds(pl.multiple_of(first, 128), ROWS)]
            pltpu.make_async_copy(block.at[pl.ds(k * RANK, RANK), :], dst, lsem.at[l_ga]).start()

    def ga_core(d, j):
        here = ga_block(d, p, j)
        copy(here, here, s_gac, r_gac + j, core).start()
        ga_store(d, p, j)

    def ga_x(d):
        here = ga_block(d, p, 0)
        for turn in range(2):
            copy(here, here, s_gax, r_gax + 3 * d + turn, xpeer(1 if turn == 0 else NX - 1)).start()
        ga_core(d, 0)

    r_tpg.wait()
    tokens = tpg[...].reshape(2 * RANK, ROWS)
    span = pl.ds(pl.multiple_of(own_slot * ROWS, 128), ROWS)
    for k in range(2):
        acc = dot(inr[k], ah[k * RANK : (k + 1) * RANK, span])
        for yy in range(NY):
            acc = acc + dot(wts[2 * yy + k], w[2 * yy + k, own_slot], NT)
        rows = slice(k * RANK, (k + 1) * RANK)
        gaf[q, x, rows, :] = (tokens[rows] - (acc[0:RANK] + acc[RANK:])).astype(BF16)
    here_ga = gaf.at[q, x]
    each(1, NY, lambda d: copy(here_ga, here_ga, s_gay, r_gay + d, ypeer(d)).start())
    ga_x(0)

    for d in (1, 3, 2):
        arrived(ga_block(d, p, 0), r_gay + d)
        ga_x(d)
    sum_products_x()
    for d in (0, 1, 3, 2):
        for turn in range(2):
            j = 1 if turn == 0 else NX - 1
            here = ga_block(d, p, j)
            arrived(here, r_gax + 3 * d + turn)
            if (d in (0, 2)) == (turn == 0):
                copy(here, here, s_gax, r_gax + 3 * d + 2, xpeer(1 if turn == 0 else NX - 1)).start()
            ga_core(d, j)
    r_ctg.wait()
    ctc[p] = ctz[...]
    s_ctc, r_ctc = sems("send"), sems("recv")
    copy(ctc.at[p], ctc.at[p], s_ctc, r_ctc, core).start()
    sent(ctc.at[p], s_ctc)
    for d in (0, 1, 3, 2):
        arrived(ga_block(d, p, 2), r_gax + 3 * d + 2)
        ga_core(d, 2)
    arrived(ctc.at[1 - p], r_ctc)
    for k in range(2):
        i = 2 * y + k
        norm_k = ns[i, 0:1]
        scal_k = ns[i, 1:2]
        gm_k = momt[pl.ds(i, 1), :]
        gm_out[k : k + 1] = gm_k
        ratio = gm_k / norm_k
        for g in range(NZ):
            gb_out[k, 4 * g : 4 * g + 4] = scal_k * (ctc[k, g, 4:8] - ctc[k, g, 0:4] * ratio)

    for j in (0, 1, 3, 2):
        arrived(gaf.at[0], r_gac + j)
        for d in range(NY):
            ga_store(d, 1 - p, j)
    arrived(gxb.at[pl.ds(0, 3 * TOK), :], r_gx)
    sent(gxb.at[pl.ds(0, 3 * TOK), :], s_gx)
    pltpu.make_async_copy(gxb.at[mine, :], gxb.at[mine, :], lsem.at[l_gx]).wait()
    sent(gaf.at[0, pl.ds(0, 3)], s_gay)
    sent(gaf.at[pl.ds(0, 3)], s_gax)
    sent(gaf.at[pl.ds(0, NY)], s_gac)
    pltpu.make_async_copy(gaf, gaf, lsem.at[l_ga]).wait()
    assert counts == limits, counts
    for final in finals:
        final()


SENDS, RECVS, LOCALS = 28, 80, 12


def finish(gx, ga, gb, gm):
    cuts = 8
    wide = NQ * HALF // cuts
    tall = TOK // 4

    def widen(gx_in, ga_in, gb_in, gm_in, gx_to, ga_to, gb_to, gm_to, narrow, full, held, sem, out_sem, gx_sem):
        def load(i):
            return pltpu.make_async_copy(ga_in.at[:, :, pl.ds(i * wide, wide)], narrow.at[i], sem.at[i])

        for i in range(cuts):
            load(i).start()
        def pick(i):
            return pltpu.make_async_copy(gx_in.at[pl.ds(i * tall, tall), :], held.at[i], gx_sem.at[i])

        for i in range(4):
            pick(i).start()
        gb_to[...] = gb_in[...]
        gm_to[...] = gm_in[...]
        for i in range(cuts):
            load(i).wait()
            full[i] = narrow[i].astype(F32)
            pltpu.make_async_copy(full.at[i], ga_to.at[:, :, pl.ds(i * wide, wide)], out_sem).start()
        for i in range(4):
            pick(i).wait()
            pltpu.make_async_copy(held.at[i], gx_to.at[pl.ds(i * tall, tall), :], gx_sem.at[4]).start()
        pltpu.make_async_copy(full, full, out_sem).wait()
        pltpu.make_async_copy(held, held, gx_sem.at[4]).wait()

    vm = pl.BlockSpec(memory_space=pltpu.VMEM)
    hbm = pl.BlockSpec(memory_space=pl.ANY)
    return pl.pallas_call(
        widen,
        out_shape=tuple(
            jax.ShapeDtypeStruct(v.shape, F32 if v is ga else v.dtype) for v in (gx, ga, gb, gm)
        ),
        in_specs=[hbm, hbm, vm, vm],
        out_specs=(hbm, hbm, vm, vm),
        scratch_shapes=[
            pltpu.VMEM((cuts, 2, RANK, wide), BF16),
            pltpu.VMEM((cuts, 2, RANK, wide), F32),
            pltpu.VMEM((4, tall, FEAT), BF16),
            pltpu.SemaphoreType.DMA((cuts,)),
            pltpu.SemaphoreType.DMA,
            pltpu.SemaphoreType.DMA((5,)),
        ],
        compiler_params=pltpu.CompilerParams(vmem_limit_bytes=62 * 2**20),
    )(gx, ga, gb, gm)


def on_device(acts, cot, base, adapter_a, adapter_b, magnitude):
    at = jnp.swapaxes(adapter_a, 1, 2)
    vm = pl.BlockSpec(memory_space=pltpu.VMEM)
    hbm = pl.BlockSpec(memory_space=pl.ANY)
    scratch = [
        ((NZ, 2, ROWS, COLS), BF16),
        ((PAIR, WORK), BF16),
        ((NQ, PAIR, COLS), BF16),
        ((NQ, PAIR, COLS), BF16),
        ((NY, 2, RANK, COLS), BF16),
        ((2 * RANK, WORK), BF16),
        ((RANK, ROWS), BF16),
        ((ROWS, COLS), BF16),
        ((NX, 8, COLS), F32),
        ((NZ, 8, COLS), F32),
        ((NQ, 8, COLS), F32),
        ((NQ, RANK, COLS), F32),
        ((NQ, RANK, COLS), F32),
        ((NZ, 8, COLS), F32),
        ((NZ, 8, COLS), F32),
        ((NX, 8, COLS), F32),
        ((NZ, 8, COLS), F32),
        ((2, NZ, 8, COLS), F32),
        ((2, 2 * RANK, ROWS), F32),
        ((2 * RANK, ROWS), F32),
        ((NZ, 8, ROWS), F32),
        ((NZ, 8, ROWS), F32),
        ((NZ, 8, ROWS), F32),
        ((NX, 8, COLS), F32),
        ((NZ, 8, COLS), F32),
        ((NQ, 8, COLS), F32),
        ((NQ, NX, 2 * RANK, ROWS), BF16),
        ((PAIR, WORK), BF16),
        ((PAIR, 2 * RANK), BF16),
        ((NQ, COLS), F32),
        ((NQ, 2 * RANK, COLS), BF16),
        ((2, 2 * RANK, RANK), BF16),
    ]
    gx, ga, gb, gm = pl.pallas_call(
        kernel,
        out_shape=(
            jax.ShapeDtypeStruct((TOK, FEAT), BF16),
            jax.ShapeDtypeStruct((2, RANK, NQ * HALF), BF16),
            jax.ShapeDtypeStruct((2, RANK, COLS), F32),
            jax.ShapeDtypeStruct((2, COLS), F32),
        ),
        in_specs=[hbm, hbm, hbm, hbm, vm, vm],
        out_specs=(hbm, hbm, vm, vm),
        scratch_shapes=[pltpu.VMEM(shape, dtype) for shape, dtype in scratch]
        + [pltpu.SemaphoreType.DMA((n,)) for n in (SENDS, RECVS, LOCALS)],
        compiler_params=pltpu.CompilerParams(
            collective_id=0, has_side_effects=True, vmem_limit_bytes=56 * 2**20
        ),
        cost_estimate=pl.CostEstimate(flops=5 * 10**9, bytes_accessed=8 * 10**6, transcendentals=0),
    )(acts, cot, base, at, adapter_b, magnitude)
    gx, ga, gb, gm = finish(gx, ga, gb, gm)
    return gx, jnp.swapaxes(ga, 1, 2), gb, gm


def solution(mesh):
    in_specs = (
        P(("dp", "fsdp"), "col"),
        P(None, ("dp", "fsdp"), "col"),
        P(None, "fsdp", "col"),
        P(),
        P(None, None, "col"),
        P(None, "col"),
    )
    out_specs = (P(("dp", "fsdp"), "col"), P(), P(None, None, "col"), P(None, "col"))
    return jax.shard_map(
        on_device, mesh=mesh, in_specs=in_specs, out_specs=out_specs, check_vma=False
    )
```

time: 101 us -> 82.9 us (0.82)
  Pallas kernels: 99.8 us -> 82 us
    pallas_call x1, Pallas kernels: 95.4 us -> 77.4 us  [on_device(): pl.pallas_call(kernel, out_shape=(jax.ShapeDtypeStruct((TOK, FEAT), BF16)...]
where the time goes in v3:
time: 82.9 us; the launch traced here: 82.6 us
  Pallas kernels  82 us (99%)
    pallas_call x1, Pallas kernels, on_device(): pl.pallas_call(kernel, out_shape=(jax.ShapeDtypeStruct((TOK, FEAT), BF16)...  77.4 us
    pallas_call x1, Pallas kernels, finish(): pl.pallas_call(widen, out_shape=tuple((jax.ShapeDtypeStruct(v.shape, F32...  4.59 us

profile of v3, /device:TPU:1, one launch (start us, length us, event | category | flops | bytes accessed | tf_op | source)
XLA Modules:
  0.0 82.6 jit_solution(17688779656212493661)
XLA Ops:
  0.6 77.4 %shard_map.93 = (bf16[192,3072]{1,0:T(8,128)(2,1)}, bf16[2,32,12288]{2,1,0:T(8,128)(2,1)}, f32[2,32,256]{2,1,0:T(8,128)}, f32[2,256]{1,0:T(2,128)}) custom-call(bf16[192,3072]{1,0:T(8,128)(2,1)} %acts.1, bf16[2,192,256]{2,1,0:T(8,128)(2,1)} %cot.1, bf16[2,384,256]{2,1,0:T(8,128)(2,1)} %base.1, bf16[2,32,12288]{2,1,0:T(8,128)(2,1)} %bitcast.3, ...), custom_call_target="tpu_custom_call" | custom-call | flops 5000000000 | bytes 8000000 | tf_op jit(solution)/shard_map/pallas_call | solution.py:716
  78.1 4.6 %shard_map.94 = (bf16[192,3072]{1,0:T(8,128)(2,1)}, f32[2,32,12288]{2,1,0:T(8,128)}, f32[2,32,256]{2,1,0:T(8,128)}, f32[2,256]{1,0:T(2,128)}) custom-call(bf16[192,3072]{1,0:T(8,128)(2,1)} %get-tuple-element.12.gx_in, bf16[2,32,12288]{2,1,0:T(8,128)(2,1)} %get-tuple-element.13.ga_in, f32[2,32,256]{2,1,0:T(8,128)} %get-tuple-element.14.gb_in, ...), custom_call_target="tpu_custom_call" | custom-call | tf_op jit(solution)/shard_map/pallas_call | solution.py:659

commit v4 on v3

--- a/solution.py
+++ b/solution.py
@@ -22,6 +22,7 @@
 ROWS = 384
 WORK = 2 * ROWS
 RANK = 32
+TILE = 128
 CUT = 160
 
 NT = (((1,), (1,)), ((), ()))
@@ -51,10 +52,10 @@
 
 def kernel(
     acts, cot, base, at, b, mag,
-    gx_out, ga_out, gb_out, gm_out,
+    gx_out, gaf, gb_out, gm_out,
     w, actsf, gf, scaled, bf, ah, ar, mybase,
     sqx, sqz, ns, tbp, tbi, ctp, cti, ctx, ctz, ctc,
-    tpp, tpi, tps, tpzi, tpg, mox, moz, moq, gaf, gxb, lowo, momt, wts, inr,
+    tpp, tpi, tps, tpzi, tpg, mox, moz, moq, gxb, lowo, momt, wts, inr,
     ssem, rsem, lsem,
 ):
     p = lax.axis_index("dp")
@@ -82,16 +83,20 @@
     own_slot = lax.div(x, 2)
     slot_of = lambda jj: lax.rem(own_slot + jj, 2)
 
-    def shift(c):
-        k, half = lax.rem(c, 2), lax.div(c, 2)
+    def turned(half, layer):
+        return lax.rem(half + lax.rem(layer, 2) * (NY - 2 * half), NY)
+
+    def shift(c, layer):
+        k, half = lax.rem(c, 2), turned(lax.div(c, 2), layer)
         return lax.rem((1 - k) * half + k * (4 + (4 - half) * jnp.minimum(half, 1)), NZ)
 
     def chunk_at(position):
         step = lax.rem(position - q + NZ, NZ)
         far = lax.div(step, 4)
-        return (1 - far) * 2 * step + far * lax.rem(17 - 2 * step, NZ)
-
-    target = (lax.rem(z, 2), lax.rem(z + shift(q), NZ) * NX + x, lax.div(z, 2))
+        c = (1 - far) * 2 * step + far * lax.rem(17 - 2 * step, NZ)
+        return 2 * turned(lax.div(c, 2), q) + lax.rem(c, 2)
+
+    target = (lax.rem(z, 2), lax.rem(z + shift(q, z), NZ) * NX + x, lax.div(z, 2))
     own = chunk_at(z)
     source = (lax.rem(own, 2), q * NX + x, lax.div(own, 2))
     fixed = jnp.logical_and(own == q, z == q)
@@ -356,6 +361,9 @@
     bx_start(0, 0)
     acts_start(1)
     cot_forward(0)
+    arrived(w.at[own, slot_of(1), pl.ds(0, CUT), :], r_ax)
+    for way in range(2):
+        z_start(0, 1, way, 0)
     r_sqz.wait()
     norms = jnp.sqrt(total(sqz, NZ)[0:1])
     ns[q, 0:1] = norms
@@ -377,8 +385,12 @@
                 z_start(0, j, way, s)
 
     def forward(zi):
-        out = dot(actsf[...], w[zi].reshape(WORK, COLS))
-        momt[pl.ds(zi, 1), :] = jnp.sum(out * gf[zi].astype(F32), axis=0, keepdims=True)
+        weight = w[zi].reshape(WORK, COLS)
+        acc = jnp.zeros((8, COLS), F32)
+        for lo in range(0, PAIR, TILE):
+            out = dot(actsf[lo : lo + TILE, :], weight)
+            acc = acc + jnp.sum((out * gf[zi, lo : lo + TILE, :].astype(F32)).reshape(TILE // 8, 8, COLS), axis=0)
+        momt[pl.ds(zi, 1), :] = jnp.sum(acc, axis=0, keepdims=True)
 
     r_tb = Ring(NQ, q, qpeer, tbi)
     r_ctz = Ring(NZ, z, zpeer, cti)
@@ -401,16 +413,20 @@
     def send_tokens():
         r_ns.wait()
         low = []
-        for k in range(2):
-            acc = None
-            for yy in range(NY):
-                i = 2 * yy + k
-                s = (gf[i].astype(F32) * ns[i, 1:2]).astype(BF16)
-                scaled[i] = s
-                t = dot(s, bf[yy, k], NT)
-                acc = t if acc is None else acc + t
-            low.append(acc)
-        lowf = jnp.concatenate(low, axis=1)
+        for lo in range(0, PAIR, TILE):
+            rows = slice(lo, lo + TILE)
+            halves = []
+            for k in range(2):
+                acc = None
+                for yy in range(NY):
+                    i = 2 * yy + k
+                    s = (gf[i, rows, :].astype(F32) * ns[i, 1:2]).astype(BF16)
+                    scaled[i, rows, :] = s
+                    t = dot(s, bf[yy, k], NT)
+                    acc = t if acc is None else acc + t
+                halves.append(acc)
+            low.append(jnp.concatenate(halves, axis=1))
+        lowf = jnp.concatenate(low, axis=0)
         lowo[...] = lowf.astype(BF16)
         lowt = lowf.T.astype(BF16)
         for j in range(2):
@@ -454,35 +470,31 @@
 
     ring_b(1)
     ring_a(0, 1)
-    arrived(w.at[own, slot_of(1), pl.ds(0, CUT), :], r_ax)
-    for way in range(2):
-        z_start(0, 1, way, 0)
     cot_relay()
+    ring_a(1, 1)
     ring_b(2)
     ring_a(0, 2)
-    ring_a(1, 1)
     r_b.wait()
     cot_relay_last()
+    ring_a(1, 2)
+    ring_b(3)
     cot_wait()
     acts_wait()
     send_tokens()
-    ring_b(3)
+    send_token_b()
     ring_a(0, 3)
+    ring_a(1, 3)
     column_sums(0, 0)
-    send_token_b()
-    ring_a(1, 2)
+    ring_b(4)
     column_sums(0, 1)
     column_sums(1, 1)
-    ring_b(4)
     ring_a(0, 4)
     column_sums(0, 2)
     column_sums(1, 2)
-    ring_a(1, 3)
+    ring_a(1, 4)
     column_sums(0, 3)
     column_sums(1, 3)
     sum_tokens_x()
-    sum_products_q()
-    ring_a(1, 4)
     bx4_wait()
     forward(origin(0, 4))
 
@@ -504,6 +516,8 @@
         for zi in range(NZ):
             acc = acc + dot(scaled[zi], w[zi, j], NT)
         gxb[:, cols] = acc.astype(BF16)
+
+    def gx_start(j):
         there = gx_out.at[:, shard(p, h, j)]
         part = pl.ds(j * ROWS, ROWS)
         for core_of, half_of, dev in ((p, 1 - h, partner), (1 - p, 1 - h, cross), (1 - p, h, core)):
@@ -511,15 +525,18 @@
         pltpu.make_async_copy(gxb.at[mine, part], there, lsem.at[l_gx]).start()
 
     backward(0)
+    gx_start(0)
+    sum_products_q()
     r_mox.wait()
     moz[z] = total(mox, NX)
     r_moz.start(lambda _: moz.at[z])
     backward(1)
     sum_tokens_z()
+    sum_products_z()
+    gx_start(1)
     r_moz.wait()
     moq[q] = total(moz, NZ)
     r_moq.start(lambda _: moq.at[q])
-    sum_products_z()
     r_moq.wait()
     moment = total(moq, NQ)
     norm_all = jnp.concatenate([ns[i, 0:1] for i in range(NQ)], axis=0)
@@ -538,30 +555,54 @@
             inner = t if inner is None else inner + t
         inr[k] = jnp.concatenate(pieces(inner[0:RANK] + inner[RANK:], 2), axis=0)
 
-    s_gay, s_gax, s_gac = sems("send"), sems("send"), sems("send")
-    r_gay, r_gax, r_gac = sems("recv", NY), sems("recv", 3 * NY), sems("recv", NX)
-    l_ga = sems("local")
-
-    def ga_block(d, of_core, j):
-        return gaf.at[2 * lax.rem(y - d + NY, NY) + of_core, lax.rem(x - j + NX, NX)]
-
-    def ga_store(d, of_core, j):
-        block = ga_block(d, of_core, j)
-        first = (2 * lax.rem(y - d + NY, NY) + of_core) * HALF + lax.rem(x - j + NX, NX) * ROWS
+    s_ga, s_gac = sems("send"), sems("send")
+    r_first, r_second, r_gac = sems("recv", NX), sems("recv", 3 * NX), sems("recv")
+
+    def ga_block(k, a, b):
+        dy, dx = (a, b) if k == 0 else (b, a)
+        block = gaf.at[2 * lax.rem(y - dy + NY, NY) + p, lax.rem(x - dx + NX, NX)]
+        return block.at[pl.ds(k * RANK, RANK), :]
+
+    def ga_peer(k, axis, d):
+        return ypeer(d) if k == axis else xpeer(d)
+
+    def ga_core(here):
+        copy(here, here, s_gac, r_gac, core).start()
+
+    def ga_second(k, a):
+        here = ga_block(k, a, 0)
+        for turn in range(2):
+            sem = r_second + 3 * a + turn
+            copy(here, here, s_ga, sem, ga_peer(k, 1, 1 if turn == 0 else 3)).start()
+        ga_core(here)
+
+    def ga_start(k):
+        here = ga_block(k, 0, 0)
+        for d in (1, 3, 2):
+            copy(here, here, s_ga, r_first + d, ga_peer(k, 0, d)).start()
+        ga_second(k, 0)
+
+    whole = gaf.at[0, 0]
+
+    def ga_first(a):
+        arrived(whole, r_first + a)
         for k in range(2):
-            dst = ga_out.at[k, :, pl.ds(pl.multiple_of(first, 128), ROWS)]
-            pltpu.make_async_copy(block.at[pl.ds(k * RANK, RANK), :], dst, lsem.at[l_ga]).start()
-
-    def ga_core(d, j):
-        here = ga_block(d, p, j)
-        copy(here, here, s_gac, r_gac + j, core).start()
-        ga_store(d, p, j)
-
-    def ga_x(d):
-        here = ga_block(d, p, 0)
+            ga_second(k, a)
+
+    def ga_forward(a):
         for turn in range(2):
-            copy(here, here, s_gax, r_gax + 3 * d + turn, xpeer(1 if turn == 0 else NX - 1)).start()
-        ga_core(d, 0)
+            arrived(whole, r_second + 3 * a + turn)
+            for k in range(2):
+                here = ga_block(k, a, 1 if turn == 0 else 3)
+                if (a in (0, 2)) == (turn == 0):
+                    sem = r_second + 3 * a + 2
+                    copy(here, here, s_ga, sem, ga_peer(k, 1, 1 if turn == 0 else 3)).start()
+                ga_core(here)
+
+    def ga_last(a):
+        arrived(whole, r_second + 3 * a + 2)
+        for k in range(2):
+            ga_core(ga_block(k, a, 2))
 
     r_tpg.wait()
     tokens = tpg[...].reshape(2 * RANK, ROWS)
@@ -572,30 +613,23 @@
             acc = acc + dot(wts[2 * yy + k], w[2 * yy + k, own_slot], NT)
         rows = slice(k * RANK, (k + 1) * RANK)
         gaf[q, x, rows, :] = (tokens[rows] - (acc[0:RANK] + acc[RANK:])).astype(BF16)
-    here_ga = gaf.at[q, x]
-    each(1, NY, lambda d: copy(here_ga, here_ga, s_gay, r_gay + d, ypeer(d)).start())
-    ga_x(0)
-
-    for d in (1, 3, 2):
-        arrived(ga_block(d, p, 0), r_gay + d)
-        ga_x(d)
+        ga_start(k)
+
     sum_products_x()
-    for d in (0, 1, 3, 2):
-        for turn in range(2):
-            j = 1 if turn == 0 else NX - 1
-            here = ga_block(d, p, j)
-            arrived(here, r_gax + 3 * d + turn)
-            if (d in (0, 2)) == (turn == 0):
-                copy(here, here, s_gax, r_gax + 3 * d + 2, xpeer(1 if turn == 0 else NX - 1)).start()
-            ga_core(d, j)
+    ga_first(1)
+    ga_first(3)
+    ga_forward(0)
+    ga_first(2)
     r_ctg.wait()
     ctc[p] = ctz[...]
     s_ctc, r_ctc = sems("send"), sems("recv")
     copy(ctc.at[p], ctc.at[p], s_ctc, r_ctc, core).start()
     sent(ctc.at[p], s_ctc)
-    for d in (0, 1, 3, 2):
-        arrived(ga_block(d, p, 2), r_gax + 3 * d + 2)
-        ga_core(d, 2)
+    ga_forward(1)
+    ga_forward(3)
+    ga_forward(2)
+    for a in (0, 1, 3, 2):
+        ga_last(a)
     arrived(ctc.at[1 - p], r_ctc)
     for k in range(2):
         i = 2 * y + k
@@ -607,71 +641,52 @@
         for g in range(NZ):
             gb_out[k, 4 * g : 4 * g + 4] = scal_k * (ctc[k, g, 4:8] - ctc[k, g, 0:4] * ratio)
 
-    for j in (0, 1, 3, 2):
-        arrived(gaf.at[0], r_gac + j)
-        for d in range(NY):
-            ga_store(d, 1 - p, j)
+    arrived(gaf.at[pl.ds(0, NY)], r_gac)
     arrived(gxb.at[pl.ds(0, 3 * TOK), :], r_gx)
     sent(gxb.at[pl.ds(0, 3 * TOK), :], s_gx)
     pltpu.make_async_copy(gxb.at[mine, :], gxb.at[mine, :], lsem.at[l_gx]).wait()
-    sent(gaf.at[0, pl.ds(0, 3)], s_gay)
-    sent(gaf.at[pl.ds(0, 3)], s_gax)
+    sent(gaf.at[pl.ds(0, 5), pl.ds(0, 3)], s_ga)
     sent(gaf.at[pl.ds(0, NY)], s_gac)
-    pltpu.make_async_copy(gaf, gaf, lsem.at[l_ga]).wait()
     assert counts == limits, counts
     for final in finals:
         final()
 
 
-SENDS, RECVS, LOCALS = 28, 80, 12
+SENDS, RECVS, LOCALS = 27, 77, 11
 
 
 def finish(gx, ga, gb, gm):
-    cuts = 8
-    wide = NQ * HALF // cuts
-    tall = TOK // 4
-
-    def widen(gx_in, ga_in, gb_in, gm_in, gx_to, ga_to, gb_to, gm_to, narrow, full, held, sem, out_sem, gx_sem):
-        def load(i):
-            return pltpu.make_async_copy(ga_in.at[:, :, pl.ds(i * wide, wide)], narrow.at[i], sem.at[i])
-
-        for i in range(cuts):
-            load(i).start()
-        def pick(i):
-            return pltpu.make_async_copy(gx_in.at[pl.ds(i * tall, tall), :], held.at[i], gx_sem.at[i])
-
-        for i in range(4):
-            pick(i).start()
+    def widen(gx_in, ga_in, gb_in, gm_in, gx_to, ga_to, gb_to, gm_to, full, gx_sem, ga_sem):
+        pltpu.make_async_copy(gx_in, gx_to, gx_sem).start()
         gb_to[...] = gb_in[...]
         gm_to[...] = gm_in[...]
-        for i in range(cuts):
-            load(i).wait()
-            full[i] = narrow[i].astype(F32)
-            pltpu.make_async_copy(full.at[i], ga_to.at[:, :, pl.ds(i * wide, wide)], out_sem).start()
-        for i in range(4):
-            pick(i).wait()
-            pltpu.make_async_copy(held.at[i], gx_to.at[pl.ds(i * tall, tall), :], gx_sem.at[4]).start()
-        pltpu.make_async_copy(full, full, out_sem).wait()
-        pltpu.make_async_copy(held, held, gx_sem.at[4]).wait()
+        for i in range(NQ):
+            for xx in range(NX):
+                for k in range(2):
+                    block = ga_in[i, xx, k * RANK : (k + 1) * RANK, :]
+                    full[i, k, :, xx * ROWS : (xx + 1) * ROWS] = block.astype(F32)
+            pltpu.make_async_copy(full.at[i], ga_to.at[:, :, pl.ds(i * HALF, HALF)], ga_sem).start()
+        pltpu.make_async_copy(full, full, ga_sem).wait()
+        pltpu.make_async_copy(gx_in, gx_in, gx_sem).wait()
 
     vm = pl.BlockSpec(memory_space=pltpu.VMEM)
     hbm = pl.BlockSpec(memory_space=pl.ANY)
     return pl.pallas_call(
         widen,
-        out_shape=tuple(
-            jax.ShapeDtypeStruct(v.shape, F32 if v is ga else v.dtype) for v in (gx, ga, gb, gm)
+        out_shape=(
+            jax.ShapeDtypeStruct(gx.shape, BF16),
+            jax.ShapeDtypeStruct((2, RANK, NQ * HALF), F32),
+            jax.ShapeDtypeStruct(gb.shape, F32),
+            jax.ShapeDtypeStruct(gm.shape, F32),
         ),
-        in_specs=[hbm, hbm, vm, vm],
+        in_specs=[vm, vm, vm, vm],
         out_specs=(hbm, hbm, vm, vm),
         scratch_shapes=[
-            pltpu.VMEM((cuts, 2, RANK, wide), BF16),
-            pltpu.VMEM((cuts, 2, RANK, wide), F32),
-            pltpu.VMEM((4, tall, FEAT), BF16),
-            pltpu.SemaphoreType.DMA((cuts,)),
+            pltpu.VMEM((NQ, 2, RANK, HALF), F32),
             pltpu.SemaphoreType.DMA,
-            pltpu.SemaphoreType.DMA((5,)),
+            pltpu.SemaphoreType.DMA,
         ],
-        compiler_params=pltpu.CompilerParams(vmem_limit_bytes=62 * 2**20),
+        compiler_params=pltpu.CompilerParams(vmem_limit_bytes=16 * 2**20),
     )(gx, ga, gb, gm)
 
 
@@ -706,7 +721,6 @@
         ((NX, 8, COLS), F32),
         ((NZ, 8, COLS), F32),
         ((NQ, 8, COLS), F32),
-        ((NQ, NX, 2 * RANK, ROWS), BF16),
         ((PAIR, WORK), BF16),
         ((PAIR, 2 * RANK), BF16),
         ((NQ, COLS), F32),
@@ -716,17 +730,17 @@
     gx, ga, gb, gm = pl.pallas_call(
         kernel,
         out_shape=(
-            jax.ShapeDtypeStruct((TOK, FEAT), BF16),
-            jax.ShapeDtypeStruct((2, RANK, NQ * HALF), BF16),
-            jax.ShapeDtypeStruct((2, RANK, COLS), F32),
-            jax.ShapeDtypeStruct((2, COLS), F32),
+            pltpu.VMEM((TOK, FEAT), BF16),
+            pltpu.VMEM((NQ, NX, 2 * RANK, ROWS), BF16),
+            pltpu.VMEM((2, RANK, COLS), F32),
+            pltpu.VMEM((2, COLS), F32),
         ),
         in_specs=[hbm, hbm, hbm, hbm, vm, vm],
-        out_specs=(hbm, hbm, vm, vm),
+        out_specs=(vm, vm, vm, vm),
         scratch_shapes=[pltpu.VMEM(shape, dtype) for shape, dtype in scratch]
         + [pltpu.SemaphoreType.DMA((n,)) for n in (SENDS, RECVS, LOCALS)],
         compiler_params=pltpu.CompilerParams(
-            collective_id=0, has_side_effects=True, vmem_limit_bytes=56 * 2**20
+            collective_id=0, has_side_effects=True, vmem_limit_bytes=58 * 2**20
         ),
         cost_estimate=pl.CostEstimate(flops=5 * 10**9, bytes_accessed=8 * 10**6, transcendentals=0),
     )(acts, cot, base, at, adapter_b, magnitude)

time: 82.9 us -> 79.8 us (0.963)
  Pallas kernels: 82 us -> 79 us
    pallas_call x2, Pallas kernels: 82 us -> 79 us  [the longest x1 76.3 us: on_device(): pl.pallas_call(kernel, out_shape=(pltpu.VMEM((TOK, FEAT), BF16), pltpu.VM...]
where the time goes in v4:
time: 79.8 us; the launch traced here: 79.7 us
  Pallas kernels  79 us (99%)
    pallas_call x1, Pallas kernels, on_device(): pl.pallas_call(kernel, out_shape=(pltpu.VMEM((TOK, FEAT), BF16), pltpu.VM...  76.3 us
    pallas_call x1, Pallas kernels, finish(): pl.pallas_call(widen, out_shape=(jax.ShapeDtypeStruct(gx.shape, BF16), ja...  2.71 us

profile of v4, /device:TPU:1, one launch (start us, length us, event | category | flops | bytes accessed | tf_op | source)
XLA Modules:
  0.0 79.7 jit_solution(15397357838891716927)
XLA Ops:
  0.6 76.3 %shard_map.93 = (bf16[192,3072]{1,0:T(8,128)(2,1)S(1)}, bf16[8,4,64,384]{3,2,1,0:T(8,128)(2,1)S(1)}, f32[2,32,256]{2,1,0:T(8,128)S(1)}, f32[2,256]{1,0:T(2,128)S(1)}) custom-call(bf16[192,3072]{1,0:T(8,128)(2,1)} %acts.1, bf16[2,192,256]{2,1,0:T(8,128)(2,1)} %cot.1, bf16[2,384,256]{2,1,0:T(8,128)(2,1)} %base.1, bf16[2,32,12288]{2,1,0:T(8,128)(2,1)} %bitcast.3, ...), custom_call_target="tpu_custom_call" | custom-call | flops 5000000000 | bytes 8000000 | tf_op jit(solution)/shard_map/pallas_call | solution.py:730
  77.0 2.7 %shard_map.94 = (bf16[192,3072]{1,0:T(8,128)(2,1)}, f32[2,32,12288]{2,1,0:T(8,128)}, f32[2,32,256]{2,1,0:T(8,128)}, f32[2,256]{1,0:T(2,128)}) custom-call(bf16[192,3072]{1,0:T(8,128)(2,1)S(1)} %get-tuple-element.12.gx_in, bf16[8,4,64,384]{3,2,1,0:T(8,128)(2,1)S(1)} %get-tuple-element.13.ga_in, f32[2,32,256]{2,1,0:T(8,128)S(1)} %get-tuple-element.14.gb_in, ...), custom_call_target="tpu_custom_call" | custom-call | tf_op jit(solution)/shard_map/pallas_call | solution.py:674

commit v5 on v4

--- a/solution.py
+++ b/solution.py
@@ -23,7 +23,7 @@
 WORK = 2 * ROWS
 RANK = 32
 TILE = 128
-CUT = 160
+CUT = 192
 
 NT = (((1,), (1,)), ((), ()))
 TN = (((0,), (0,)), ((), ()))
@@ -349,7 +349,6 @@
     r_sqx.wait()
     sqz[z] = total(sqx, NX)
     r_sqz.start(lambda _: sqz.at[z])
-    cot_start()
     wait_swap(1)
     for way in range(2):
         z_start(1, 0, way, 0)
@@ -359,6 +358,7 @@
     for way in range(2):
         z_start(0, 0, way, 0)
     bx_start(0, 0)
+    cot_start()
     acts_start(1)
     cot_forward(0)
     arrived(w.at[own, slot_of(1), pl.ds(0, CUT), :], r_ax)
@@ -620,14 +620,14 @@
     ga_first(3)
     ga_forward(0)
     ga_first(2)
+    ga_forward(1)
+    ga_forward(3)
+    ga_forward(2)
     r_ctg.wait()
     ctc[p] = ctz[...]
     s_ctc, r_ctc = sems("send"), sems("recv")
     copy(ctc.at[p], ctc.at[p], s_ctc, r_ctc, core).start()
     sent(ctc.at[p], s_ctc)
-    ga_forward(1)
-    ga_forward(3)
-    ga_forward(2)
     for a in (0, 1, 3, 2):
         ga_last(a)
     arrived(ctc.at[1 - p], r_ctc)

time: 79.8 us -> 79.7 us (level)
  no operation moved by 1% of the time
where the time goes in v5:
time: 79.7 us; the launch traced here: 79.6 us
  Pallas kernels  79 us (99%)
    pallas_call x1, Pallas kernels, on_device(): pl.pallas_call(kernel, out_shape=(pltpu.VMEM((TOK, FEAT), BF16), pltpu.VM...  76.2 us
    pallas_call x1, Pallas kernels, finish(): pl.pallas_call(widen, out_shape=(jax.ShapeDtypeStruct(gx.shape, BF16), ja...  2.71 us

profile of v5, /device:TPU:1, one launch (start us, length us, event | category | flops | bytes accessed | tf_op | source)
XLA Modules:
  0.0 79.6 jit_solution(9179068065414483395)
XLA Ops:
  0.6 76.2 %shard_map.93 = (bf16[192,3072]{1,0:T(8,128)(2,1)S(1)}, bf16[8,4,64,384]{3,2,1,0:T(8,128)(2,1)S(1)}, f32[2,32,256]{2,1,0:T(8,128)S(1)}, f32[2,256]{1,0:T(2,128)S(1)}) custom-call(bf16[192,3072]{1,0:T(8,128)(2,1)} %acts.1, bf16[2,192,256]{2,1,0:T(8,128)(2,1)} %cot.1, bf16[2,384,256]{2,1,0:T(8,128)(2,1)} %base.1, bf16[2,32,12288]{2,1,0:T(8,128)(2,1)} %bitcast.3, ...), custom_call_target="tpu_custom_call" | custom-call | flops 5000000000 | bytes 8000000 | tf_op jit(solution)/shard_map/pallas_call | solution.py:730
  76.9 2.7 %shard_map.94 = (bf16[192,3072]{1,0:T(8,128)(2,1)}, f32[2,32,12288]{2,1,0:T(8,128)}, f32[2,32,256]{2,1,0:T(8,128)}, f32[2,256]{1,0:T(2,128)}) custom-call(bf16[192,3072]{1,0:T(8,128)(2,1)S(1)} %get-tuple-element.12.gx_in, bf16[8,4,64,384]{3,2,1,0:T(8,128)(2,1)S(1)} %get-tuple-element.13.ga_in, f32[2,32,256]{2,1,0:T(8,128)S(1)} %get-tuple-element.14.gb_in, ...), custom_call_target="tpu_custom_call" | custom-call | tf_op jit(solution)/shard_map/pallas_call | solution.py:674
